TPU v7x, 256 devices: a whole 4x4x8 slice. The times are simulated.
256 devices in a mesh: stream: 32 (over y_hi, z, core), et: 8 (over x, y_lo).
Axes of the slice: x: 4, y: 4 (y_hi: 2, y_lo: 2; y = y_hi * 2 + y_lo), z: 8, core: 2. Of those that a mesh axis runs over, the one named last changes fastest.
Arguments:
- residual_in: bfloat16 [512, 2048], P('stream', 'et'), may hold values from -3 to 3
- attn_gain: bfloat16 [2048], replicated, may hold values from 0.099609375 to 1.8984375
- q_gain: bfloat16 [128], replicated, may hold values from 0.099609375 to 1.8984375
- key_norm_gain: bfloat16 [128], replicated, may hold values from 0.099609375 to 1.8984375
- w_q: bfloat16 [2048, 4096], P(None, 'et'), may hold values from -0.125 to 0.125
- key_value_weight: bfloat16 [2048, 1024], P(None, 'et'), may hold values from -0.125 to 0.125
- w_o: bfloat16 [4096, 2048], P(None, 'et'), may hold values from -0.09375 to 0.09375
- key_value_cache: bfloat16 [512, 768, 2, 512], P(('stream', 'et')), may hold values from -4 to 4
- cache_length: int32 [512], P('stream'), may hold values from 1 to 768, as said below
- moe_gain: bfloat16 [2048], P('et'), may hold values from 0.099609375 to 1.8984375
- route_ids: int32 [512, 8], P('stream'), may hold values from 0 to 127, all different within a row; in each aligned block of 16 rows (0 to 15, 16 to 31, ...) at most 2 rows name the same one
- route_gates: float32 [512, 8], P('stream'), may hold values from 0.05 to 1
- w_gate_up: bfloat16 [128, 2, 2048, 768], P('stream', None, 'et'), may hold values from -0.125 to 0.125
- w_down: bfloat16 [128, 768, 2048], P('stream', None, 'et'), may hold values from -0.21875 to 0.21875
Outputs:
- layer_out: bfloat16 [512, 2048], P('stream', 'et')
Inputs may be any that keep to these rules, and one draw needn't show every extreme that they name: `route_ids`: each row names 8 different experts. Within each aligned block of 16 rows no expert is named more than 2 times, a bound that some block reaches. `cache_length`: some stream holds exactly 768 cached positions.
All inputs are finite; a program needn't handle non-finite values.
Results may differ from a plain program's by a relative error of at most 0.02.
Values may be sent and summed in bfloat16 or wider, within the bound.
A program may use at most 64 MiB of HBM per device.

v0:
```python
import jax
import jax.numpy as jnp
from jax import lax
from jax.sharding import PartitionSpec as P

CAP = 2


EPS = 1e-06
ROPE_BASE = 1000000.0


def per_head_norm(value_rows, gain):
    return (
        value_rows
        * lax.rsqrt(jnp.mean(value_rows * value_rows, axis=-1, keepdims=True) + EPS)
        * gain.astype(jnp.float32)
    )


def rotary_embed(value_rows, positions):
    half = value_rows.shape[-1] // 2
    steps = jnp.arange(half).astype(jnp.float32)
    freq = ROPE_BASE ** (-(2.0 * steps) / value_rows.shape[-1])
    angle = positions.astype(jnp.float32)[:, None, None] * freq
    cosine = jnp.cos(angle)
    sine = jnp.sin(angle)
    lower = value_rows[..., :half]
    upper = value_rows[..., half:]
    return jnp.concatenate([lower * cosine - upper * sine, upper * cosine + lower * sine], axis=-1)


def on_device(
    residual_in,
    attn_gain,
    q_gain,
    key_norm_gain,
    w_q,
    key_value_weight,
    w_o,
    key_value_cache,
    cache_length,
    moe_gain,
    route_ids,
    route_gates,
    w_gate_up,
    w_down,
):
    n_et = lax.axis_size("et")
    n_stream = lax.axis_size("stream")
    et_pos = lax.axis_index("et")
    input_rows = residual_in.shape[0]
    head_dim = q_gain.shape[0]
    kv_heads = key_value_cache.shape[3] // head_dim
    span = key_value_cache.shape[1]
    local = key_value_cache.shape[0]
    full_input = lax.all_gather(residual_in, "et", axis=1, tiled=True)
    full_f = full_input.astype(jnp.float32)
    normed_input = (
        full_f
        * lax.rsqrt(jnp.mean(full_f * full_f, axis=-1, keepdims=True) + EPS)
        * attn_gain.astype(jnp.float32)
    ).astype(jnp.bfloat16)
    own_query = jnp.dot(normed_input, w_q, preferred_element_type=jnp.float32).reshape(
        input_rows, -1, head_dim
    )
    own_query = rotary_embed(per_head_norm(own_query, q_gain), cache_length).astype(jnp.bfloat16)
    own_kv = jnp.dot(normed_input, key_value_weight, preferred_element_type=jnp.float32).reshape(
        input_rows, -1, head_dim
    )
    blocks = own_kv.shape[1]
    block_ids = et_pos * blocks + jnp.arange(blocks)
    is_key = (block_ids < kv_heads)[None, :, None]
    own_kv = jnp.where(
        is_key, rotary_embed(per_head_norm(own_kv, key_norm_gain), cache_length), own_kv
    ).astype(jnp.bfloat16)
    all_query, all_kv = (
        lax.all_to_all(
            own_query.reshape(input_rows, -1), "et", split_axis=0, concat_axis=1, tiled=True
        ),
        lax.all_to_all(
            own_kv.reshape(input_rows, -1), "et", split_axis=0, concat_axis=1, tiled=True
        ),
    )
    q_heads = all_query.shape[1] // head_dim
    query_group = q_heads // kv_heads
    scale = head_dim ** (-0.5)
    lengths = lax.dynamic_slice_in_dim(cache_length, et_pos * local, local, 0)
    query_vector = all_query.reshape(local, kv_heads, query_group, head_dim)
    key_rows = key_value_cache[:, :, 0].reshape(local, span, kv_heads, head_dim)
    value_rows = key_value_cache[:, :, 1].reshape(local, span, kv_heads, head_dim)
    scores = (
        jnp.einsum("shgd,slhd->shgl", query_vector, key_rows, preferred_element_type=jnp.float32)
        * scale
    )
    live = (jnp.arange(span)[None, :] < lengths[:, None])[:, None, None, :]
    weights = jnp.where(live, jnp.exp(scores), 0.0)
    total = jnp.sum(weights, axis=-1)
    summed = jnp.einsum(
        "shgl,slhd->shgd",
        weights.astype(jnp.bfloat16),
        value_rows,
        preferred_element_type=jnp.float32,
    )
    new_keys = (
        all_kv[:, : kv_heads * head_dim].reshape(local, kv_heads, 1, head_dim).astype(jnp.float32)
    )
    new_values = (
        all_kv[:, kv_heads * head_dim :].reshape(local, kv_heads, 1, head_dim).astype(jnp.float32)
    )
    fresh = jnp.exp(jnp.sum(query_vector.astype(jnp.float32) * new_keys, axis=-1) * scale)
    summed = summed + fresh[..., None] * new_values
    total = total + fresh
    mixed_local = (summed / total[..., None]).astype(jnp.bfloat16).reshape(local, -1)
    attention_mixed = lax.all_gather(mixed_local, "et", axis=0, tiled=True)
    resid = (
        residual_in.astype(jnp.float32)
        + jnp.dot(attention_mixed, w_o, preferred_element_type=jnp.float32)
    ).astype(jnp.bfloat16)
    resid_f = resid.astype(jnp.float32)
    squares = lax.psum(jnp.sum(resid_f * resid_f, axis=-1), "et")
    width = resid_f.shape[1] * n_et
    expert_in = (
        resid_f * lax.rsqrt(squares / width + EPS)[:, None] * moe_gain.astype(jnp.float32)
    ).astype(jnp.bfloat16)
    top_count = route_ids.shape[1]
    local_experts = w_gate_up.shape[0]
    experts = local_experts * n_stream
    slots_all = experts * CAP
    flat_ids = route_ids.reshape(-1)
    onehot = (flat_ids[:, None] == jnp.arange(experts)[None, :]).astype(jnp.int32)
    earlier = jnp.cumsum(onehot, axis=0) - onehot
    slot = jnp.sum(earlier * onehot, axis=1)
    target = flat_ids * CAP + slot
    placing = (jnp.arange(slots_all)[:, None] == target[None, :]).astype(jnp.float32)
    token_place = jnp.sum(placing.reshape(slots_all, input_rows, top_count), axis=-1)
    outgoing = jnp.dot(
        token_place.astype(jnp.bfloat16), expert_in, preferred_element_type=jnp.float32
    ).astype(jnp.bfloat16)
    received = lax.all_to_all(outgoing, "stream", split_axis=0, concat_axis=0, tiled=True)
    grid = received.reshape(n_stream, local_experts, CAP, -1)
    partial_value = jnp.einsum(
        "secd,egdf->secgf", grid, w_gate_up, preferred_element_type=jnp.float32
    )
    pair = lax.psum(partial_value, "et")
    hidden = (jax.nn.silu(pair[..., 0, :]) * pair[..., 1, :]).astype(jnp.bfloat16)
    out_rows = jnp.einsum(
        "secf,efd->secd", hidden, w_down, preferred_element_type=jnp.float32
    ).astype(jnp.bfloat16)
    returned = lax.all_to_all(
        out_rows.reshape(slots_all, -1), "stream", split_axis=0, concat_axis=0, tiled=True
    )
    gate_weight = route_gates / jnp.sum(route_gates, axis=-1, keepdims=True)
    mixing = jnp.sum(
        (placing * gate_weight.reshape(-1)[None, :]).reshape(slots_all, input_rows, top_count),
        axis=-1,
    )
    routed = jnp.dot(mixing.T, returned.astype(jnp.float32), precision=lax.Precision.HIGHEST)
    return (resid_f + routed).astype(jnp.bfloat16)


def solution(mesh):
    placed = (
        P("stream", "et"),
        P(),
        P(),
        P(),
        P(None, "et"),
        P(None, "et"),
        P(None, "et"),
        P(("stream", "et"), None, None, None),
        P("stream"),
        P("et"),
        P("stream", None),
        P("stream", None),
        P("stream", None, "et", None),
        P("stream", None, "et"),
    )
    return jax.shard_map(
        on_device, mesh=mesh, in_specs=placed, out_specs=P("stream", "et"), check_vma=False
    )
```

profile of v0, /device:TPU:1, one launch (start us, length us, event | category | flops | bytes accessed | tf_op | source)
XLA Modules:
  0.0 276.8 jit_solution(15631513456078278853)
XLA Ops:
  6.5 0.0 copy-start
  6.5 23.4 %all_gather.6 = bf16[16,2048]{1,0:T(8,128)(2,1)S(1)} all-gather(bf16[16,256]{1,0:T(8,128)(2,1)} %param.14), channel_id=1, replica_groups=mesh['stream'=32,'et'=8] {'et'}, dimensions={1}, use_global_device_ids=true | all-gather | bytes 73728 | tf_op jit(solution)/shard_map/all_gather | solution.py:57
  29.9 0.7 convert_element_type.113
  30.6 0.1 fusion.22
  30.7 0.7 convert_element_type.116
  31.4 0.7 convert_element_type.121
  32.1 1.4 multiply_reduce_fusion.3
  33.5 0.1 multiply_bitcast_fusion
  33.5 0.1 fusion.37
  33.7 0.7 fusion.40
  34.3 4.4 %all-to-all-start.1 = ((bf16[8,2,128]{2,1,0:T(2,128)(2,1)}), bf16[8,2,128]{2,1,0:T(2,128)(2,1)S(1)}, u32[]{:S(2)}, u32[]{:S(2)}) async-start(bf16[8,2,128]{2,1,0:T(2,128)(2,1)} %bitcast.6), calls=%async_computation.1 | async-start | bytes 8192 | tf_op jit(solution)/shard_map/all_to_all | solution.py:81
  38.7 0.1 multiply_cosine_fusion.1
  38.8 0.0 copy-start.1
  38.8 9.5 %fusion.46 = (bf16[2,768,1,512]{3,2,1,0:T(2,128)(2,1)}, bf16[2,768,1,512]{3,2,1,0:T(2,128)(2,1)}) fusion(bf16[2,768,2,512]{3,2,1,0:T(2,128)(2,1)} %param.21), kind=kLoop, calls=%fused_computation.79 | loop fusion | bytes 6291456 | tf_op jit(solution)/shard_map/slice | solution.py:90
  48.3 0.0 copy-done.1
  48.3 0.0 copy-start.5
  48.3 0.0 copy-start.6
  48.3 0.0 copy-start.4
  48.3 0.0 copy-start.3
  48.4 0.4 fusion.30
  48.8 0.2 copy-done.5
  49.0 0.1 multiply_reduce_fusion.1
  49.1 0.0 copy-done.6
  49.1 0.1 dynamic_slice.3
  49.2 0.1 iota_compare_fusion.2
  49.3 0.0 copy-done.4
  49.3 0.1 copy.48
  49.3 0.1 eq.31
  49.4 0.1 fusion.27
  49.5 0.2 reduce_window_sum.11
  49.7 0.2 select_reduce_fusion.1
  49.9 0.1 reduce_sum.98
  50.0 0.0 copy-done.3
  50.0 0.1 copy.50
  50.1 0.1 multiply_multiply_fusion
  50.2 0.1 convert_reduce_fusion
  50.3 0.1 subtract_convert_fusion
  50.4 0.1 pad_maximum_fusion
  50.5 8.2 %copy.60 = bf16[2,768,1,512]{1,3,0,2:T(8,128)(2,1)} copy(bf16[2,768,1,512]{3,2,1,0:T(2,128)(2,1)} %get-tuple-element.8) | data formatting | bytes 3145728
  58.7 0.6 convert_element_type.118
  59.4 8.2 %copy.59 = bf16[2,768,1,512]{1,3,0,2:T(8,128)(2,1)} copy(bf16[2,768,1,512]{3,2,1,0:T(2,128)(2,1)} %get-tuple-element.7) | data formatting | bytes 3145728
  67.5 0.0 copy-done.7
  67.5 0.0 all-to-all-done.1
  67.5 5.2 %all-to-all-start = ((bf16[8,2,512]{2,1,0:T(2,128)(2,1)}), bf16[8,2,512]{2,1,0:T(2,128)(2,1)S(1)}, u32[]{:S(2)}, u32[]{:S(2)}) async-start(bf16[8,2,512]{2,1,0:T(2,128)(2,1)} %convert_element_type.118), calls=%async_computation | async-start | bytes 32768 | tf_op jit(solution)/shard_map/all_to_all | solution.py:78
  72.7 0.0 all-reduce.2.cloned.1.call-start
  72.8 5.0 %all-to-all-done = bf16[8,2,512]{2,1,0:T(2,128)(2,1)S(1)} async-done(((bf16[8,2,512]{2,1,0:T(2,128)(2,1)}), bf16[8,2,512]{2,1,0:T(2,128)(2,1)S(1)}, u32[]{:S(2)}, u32[]{:S(2)}) %all-to-all-start) | async-done | bytes 16416 | tf_op jit(solution)/shard_map/all_to_all | solution.py:78
  77.8 0.1 multiply_reduce_fusion
  77.9 1.8 fusion.47
  79.7 1.9 fusion.14
  81.6 21.8 %all-gather = bf16[8,2,4096]{2,1,0:T(2,128)(2,1)S(1)} all-gather(bf16[1,2,4096]{2,1,0:T(2,128)(2,1)S(1)} %reshape.278), channel_id=1, replica_groups=mesh['stream'=32,'et'=8] {'et'}, dimensions={0}, use_global_device_ids=true | all-gather | bytes 147456 | tf_op jit(solution)/shard_map/all_gather | solution.py:115
  103.5 0.1 reshape.279
  103.5 0.0 copy-done.2
  103.5 2.1 multiply_reduce_fusion.2
  105.6 13.4 %psum.14 = f32[16]{0:T(128)S(1)} all-reduce(f32[16]{0:T(128)S(1)} %get-tuple-element.23), channel_id=1, replica_groups=mesh['stream'=32,'et'=8] {'et'}, use_global_device_ids=true, to_apply=%region_11.12 | all-reduce | flops 16 | bytes 128 | tf_op jit(solution)/shard_map/psum | solution.py:121
  119.1 0.2 fusion.12
  119.3 40.5 %all_to_all.53 = bf16[32,8,256]{2,1,0:T(8,128)(2,1)S(1)} all-to-all(bf16[32,8,256]{2,1,0:T(8,128)(2,1)S(1)} %fusion.12), channel_id=1, replica_groups=mesh['stream'=32,'et'=8] {'stream'}, dimensions={0} | all-to-all | bytes 262144 | tf_op jit(solution)/shard_map/all_to_all | solution.py:140
  159.8 0.0 copy-done
  159.8 1.8 fusion.4
  161.6 0.0 all-reduce.2.cloned.1.call-update
  161.6 82.6 %all-reduce.2.cloned.1.call-done = f32[32,4,2,2,768]{4,0,3,2,1:T(8,128)} async-done(((f32[32,4,2,2,768]{4,0,3,2,1:T(8,128)}), f32[32,4,2,2,768]{4,0,3,2,1:T(8,128)}) %all-reduce.2.cloned.1.call-update) | async-done | bytes 1572880 | tf_op jit(solution)/shard_map/psum | solution.py:145
  244.3 2.3 fusion.9
  246.6 0.1 copy.53
  246.7 22.5 %all_to_all.54 = bf16[32,8,256]{2,1,0:T(8,128)(2,1)S(1)} all-to-all(bf16[32,8,256]{2,1,0:T(8,128)(2,1)S(1)} %copy.53), channel_id=1, replica_groups=mesh['stream'=32,'et'=8] {'stream'}, dimensions={0} | all-to-all | bytes 262144 | tf_op jit(solution)/shard_map/all_to_all | solution.py:150
  269.2 0.8 fusion.17
  (21 shorter events, 0.2 us)
Async XLA Ops:
  6.5 153.3 %copy-start = (bf16[4,2,256,768]{3,2,1,0:T(8,128)(2,1)S(1)}, bf16[4,2,256,768]{3,2,1,0:T(8,128)(2,1)}, u32[]{:S(2)}) copy-start(bf16[4,2,256,768]{3,2,1,0:T(8,128)(2,1)} %param.26) | copy-start | bytes 9437188
  34.3 33.2 %all-to-all-start.1 = ((bf16[8,2,128]{2,1,0:T(2,128)(2,1)}), bf16[8,2,128]{2,1,0:T(2,128)(2,1)S(1)}, u32[]{:S(2)}, u32[]{:S(2)}) async-start(bf16[8,2,128]{2,1,0:T(2,128)(2,1)} %bitcast.6), calls=%async_computation.1 | async-start | bytes 8192 | tf_op jit(solution)/shard_map/all_to_all | solution.py:81
  38.8 9.5 %copy-start.1 = (bf16[2048,512]{1,0:T(8,128)(2,1)S(1)}, bf16[2048,512]{1,0:T(8,128)(2,1)}, u32[]{:S(2)}) copy-start(bf16[2048,512]{1,0:T(8,128)(2,1)} %param.18) | copy-start | bytes 6291460
  48.3 0.7 copy-start.5
  48.3 0.8 copy-start.6
  48.3 0.9 copy-start.4
  48.3 1.6 copy-start.3
  59.3 8.2 %copy-start.7 = (bf16[256]{0:T(256)(128)(2,1)S(1)}, bf16[256]{0:T(256)(128)(2,1)}, u32[]{:S(2)}) copy-start(bf16[256]{0:T(256)(128)(2,1)} %param.23) | copy-start | bytes 1540
  67.5 36.0 %copy-start.2 = (bf16[16,256]{1,0:T(8,128)(2,1)S(1)}, bf16[16,256]{1,0:T(8,128)(2,1)}, u32[]{:S(2)}) copy-start(bf16[16,256]{1,0:T(8,128)(2,1)} %param.14) | copy-start | bytes 24580
  67.5 10.2 %all-to-all-start = ((bf16[8,2,512]{2,1,0:T(2,128)(2,1)}), bf16[8,2,512]{2,1,0:T(2,128)(2,1)S(1)}, u32[]{:S(2)}, u32[]{:S(2)}) async-start(bf16[8,2,512]{2,1,0:T(2,128)(2,1)} %convert_element_type.118), calls=%async_computation | async-start | bytes 32768 | tf_op jit(solution)/shard_map/all_to_all | solution.py:78
  72.7 171.6 %all-reduce.2.cloned.1.call-start = ((), (), s32[]{:S(2)}) async-start(), calls=%async_computation.4 | async-start | bytes 3145728 | tf_op jit(solution)/shard_map/psum | solution.py:145
Sparse Core Ops, SparseCore 0:
  161.8 82.4 all-reduce.1
where the time goes:
time: 278 us; the launch traced here: 277 us
  blocking collectives  122 us (44%)
  waiting for transfers between devices  87.6 us (32%)
  local copies, waits for them, and re-layouts  27.3 us (10%)
  between operations  13.7 us (5%)
  matrix products  12.8 us (5%)
  starting transfers between devices  9.55 us (3%)
  other arithmetic  4.33 us (2%)
    psum x1, waiting for transfers between devices, on_device(): pair = lax.psum(partial_value, 'et')  82.6 us
    all_to_all x1, blocking collectives, on_device(): lax.all_to_all(outgoing, 'stream', split_axis=0, concat_axis=0, tiled=True)  40.5 us
    all_gather x1, blocking collectives, on_device(): full_input = lax.all_gather(residual_in, 'et', axis=1, tiled=True)  23.4 us
    all_to_all x1, blocking collectives, on_device(): lax.all_to_all(out_rows.reshape(slots_all, -1), 'stream', split_axis=0, c...  22.5 us
    all_gather x1, blocking collectives, on_device(): attention_mixed = lax.all_gather(mixed_local, 'et', axis=0, tiled=True)  21.8 us
    unnamed x21, local copies, waits for them, and re-layouts  16.7 us
    psum x1, blocking collectives, on_device(): squares = lax.psum(jnp.sum(resid_f * resid_f, axis=-1), 'et')  13.4 us
    slice x1, local copies, waits for them, and re-layouts, on_device(): key_rows = key_value_cache[:, :, 0].reshape(local, span, kv_heads, head_dim)  9.47 us
  transfers between devices with their start and end apart: 3, of which 2 were waited for; matrix products, arithmetic and copies ran while one was open for 10% of the time, Pallas kernels for 0%

commit v1 on v0

v1 whole, which is shorter than its diff:
```python
import functools
import math

import jax
import jax.numpy as jnp
from jax import lax
from jax.experimental import pallas as pl
from jax.experimental.pallas import tpu as pltpu
from jax.sharding import PartitionSpec as P

EPS = 1e-06
ROPE_BASE = 1000000.0
CAP = 2
LANES = 128
MESH = pl.DeviceIdType.MESH
F32 = jnp.float32
BF16 = jnp.bfloat16

FEATURES, HEADS, MIXED, PAIRS, HIDDEN = range(5)
OUTWARD, HOME = range(2)


def iota(shape, dim):
    return lax.broadcasted_iota(jnp.int32, shape, dim)


def dot(a, b):
    return jnp.dot(a, b, preferred_element_type=F32)


def dot_nt(a, b):
    return lax.dot_general(a, b, (((1,), (1,)), ((), ())), preferred_element_type=F32)


def dot_tn(a, b):
    return lax.dot_general(a, b, (((0,), (0,)), ((), ())), preferred_element_type=F32)


def kernel(
    n_stream,
    n_et,
    res_hbm,
    attn_gain_hbm,
    q_gain_hbm,
    key_gain_hbm,
    w_q_hbm,
    w_kv_hbm,
    w_o_hbm,
    cache_hbm,
    length_hbm,
    moe_gain_hbm,
    ids_hbm,
    gates_hbm,
    w_gu_hbm,
    w_down_hbm,
    out_ref,
    attn_gain,
    q_gain,
    key_gain,
    w_q,
    w_kv,
    w_o,
    cache,
    length,
    moe_gain,
    ids,
    gates,
    w_gu,
    w_down,
    features,
    heads_out,
    heads_in,
    mixed_out,
    mixed_in,
    mixed_f,
    rows_out,
    rows_in,
    rows_f,
    expert_rows,
    expert_squares,
    pairs_out,
    pairs_own,
    pairs_in,
    hidden_out,
    hidden_in,
    results_f,
    results_out,
    results_in,
    load_sem,
    et_send,
    et_recv,
    stream_send,
    stream_recv,
):
    me_s = lax.axis_index("stream")
    me = lax.axis_index("et")
    tokens = res_hbm.shape[0]
    local = tokens // n_et
    head_dim = q_gain_hbm.shape[1]
    own_heads = w_q_hbm.shape[1] // head_dim
    n_heads = own_heads * n_et
    kv_heads = n_et // 2
    group = n_heads // kv_heads
    width = res_hbm.shape[1] * n_et
    n_local = w_gu_hbm.shape[0]
    slots = n_stream * n_local * CAP
    scale = head_dim**-0.5

    loads = {}
    for name, source, target in (
        ("own", res_hbm, features.at[me]),
        ("length", length_hbm, length),
        ("attn_gain", attn_gain_hbm, attn_gain),
        ("q_gain", q_gain_hbm, q_gain),
        ("key_gain", key_gain_hbm, key_gain),
        ("ids", ids_hbm, ids),
        ("gates", gates_hbm, gates),
        ("moe_gain", moe_gain_hbm, moe_gain),
        ("w_q", w_q_hbm, w_q),
        ("w_kv", w_kv_hbm, w_kv),
        ("cache", cache_hbm, cache),
        ("w_o", w_o_hbm, w_o),
        ("w_gu", w_gu_hbm, w_gu),
        ("w_down", w_down_hbm, w_down),
    ):
        loads[name] = pltpu.make_async_copy(source, target, load_sem.at[len(loads)])
        loads[name].start()

    def et_peer(step):
        return lax.rem(me + step, n_et)

    def stream_peer(step):
        return lax.rem(me_s + step, n_stream)

    def et_copy(exchange, source, target, peer):
        return pltpu.make_async_remote_copy(
            src_ref=source,
            dst_ref=target,
            send_sem=et_send.at[exchange, peer],
            recv_sem=et_recv.at[exchange, me],
            device_id=(me_s, peer),
            device_id_type=MESH,
        )

    def et_arrival(exchange, source, target, peer):
        return pltpu.make_async_remote_copy(
            src_ref=source,
            dst_ref=target,
            send_sem=et_send.at[exchange, peer],
            recv_sem=et_recv.at[exchange, peer],
            device_id=(me_s, peer),
            device_id_type=MESH,
        )

    def stream_copy(exchange, source, target, peer):
        return pltpu.make_async_remote_copy(
            src_ref=source,
            dst_ref=target,
            send_sem=stream_send.at[exchange, peer],
            recv_sem=stream_recv.at[exchange, me_s],
            device_id=(peer, me),
            device_id_type=MESH,
        )

    def stream_arrival(exchange, source, target, peer):
        return pltpu.make_async_remote_copy(
            src_ref=source,
            dst_ref=target,
            send_sem=stream_send.at[exchange, peer],
            recv_sem=stream_recv.at[exchange, peer],
            device_id=(peer, me),
            device_id_type=MESH,
        )

    def loop(n, body):
        def step(i, carry):
            body(i)
            return carry

        lax.fori_loop(1, n, step, 0)

    barrier = pltpu.get_barrier_semaphore()
    loop(
        n_et,
        lambda i: pl.semaphore_signal(
            barrier, inc=1, device_id=(me_s, et_peer(i)), device_id_type=MESH
        ),
    )
    loop(
        n_stream,
        lambda i: pl.semaphore_signal(
            barrier, inc=1, device_id=(stream_peer(i), me), device_id_type=MESH
        ),
    )
    pl.semaphore_wait(barrier, n_et + n_stream - 2)

    loop(
        n_et,
        lambda i: et_copy(FEATURES, res_hbm, features.at[me], et_peer(i)).start(),
    )

    loads["length"].wait()
    lengths = jnp.broadcast_to(length[...], (tokens, tokens)).astype(F32)
    diagonal = iota((tokens, tokens), 0) == iota((tokens, tokens), 1)
    positions = jnp.sum(jnp.where(diagonal, lengths, 0.0), axis=1, keepdims=True)
    half = head_dim // 2
    lane = iota((tokens, head_dim), 1)
    steps = jnp.where(lane < half, lane, lane - half).astype(F32)
    angle = positions * jnp.exp(steps * (-2.0 * math.log(ROPE_BASE) / head_dim))
    cosine = jnp.cos(angle)
    sine = jnp.where(lane < half, -jnp.sin(angle), jnp.sin(angle))

    pad = 16
    row = iota((n_et * pad, LANES), 0)
    col = iota((n_et * pad, LANES), 1)
    peer_of, at = lax.div(row, pad), lax.rem(row, pad)
    n_q = local * own_heads
    picked = jnp.where(
        at < n_q,
        lax.rem(at, own_heads) * tokens + peer_of * local + lax.div(at, own_heads),
        jnp.where(
            at < n_q + local, own_heads * tokens + peer_of * local + at - n_q, -1
        ),
    )
    order_out = jnp.where(col == picked, 1.0, 0.0).astype(BF16)

    per = local * n_heads
    row = iota((3 * per, n_et * pad), 0)
    col = iota((3 * per, n_et * pad), 1)
    kind, at = lax.div(row, per), lax.rem(row, per)
    token, head = lax.div(at, n_heads), lax.rem(at, n_heads)
    picked = jnp.where(
        kind == 0,
        lax.div(head, own_heads) * pad + token * own_heads + lax.rem(head, own_heads),
        (lax.div(head, group) + jnp.where(kind == 2, kv_heads, 0)) * pad + n_q + token,
    )
    order_in = jnp.where(col == picked, 1.0, 0.0).astype(BF16)

    loads["ids"].wait()
    loads["gates"].wait()
    at = iota((slots, tokens), 0)
    place = lax.rem(at, n_local * CAP)
    expert = lax.div(at, n_local * CAP) * n_local + lax.rem(place, n_local)
    which = lax.div(place, n_local)
    gate = gates[...]
    gate = gate / jnp.sum(gate, axis=0, keepdims=True)
    named = jnp.zeros((slots, tokens), F32)
    weight = jnp.zeros((slots, tokens), F32)
    for k in range(ids_hbm.shape[0]):
        hit = expert == ids[k : k + 1, :]
        named = jnp.where(hit, 1.0, named)
        weight = jnp.where(hit, gate[k : k + 1, :], weight)
    before = jnp.where(
        iota((tokens, tokens), 0) < iota((tokens, tokens), 1), 1.0, 0.0
    ).astype(BF16)
    earlier = dot(named.astype(BF16), before)
    placed = jnp.where(earlier == which.astype(F32), named, 0.0)
    mixing = placed * weight
    placed = placed.astype(BF16)
    mixing_high = mixing.astype(BF16)
    mixing_low = (mixing - mixing_high.astype(F32)).astype(BF16)

    loads["own"].wait()
    loads["attn_gain"].wait()
    loop(
        n_et,
        lambda i: et_arrival(
            FEATURES, res_hbm, features.at[et_peer(i)], et_peer(i)
        ).wait_recv(),
    )
    full = jnp.concatenate([features[i].astype(F32) for i in range(n_et)], axis=1)
    gain = attn_gain[...].astype(F32)
    gain = jnp.concatenate([gain[i : i + 1] for i in range(gain.shape[0])], axis=1)
    normed = (
        full
        * lax.rsqrt(jnp.sum(full * full, axis=1, keepdims=True) * (1.0 / width) + EPS)
        * gain
    ).astype(BF16)

    def rotated(v, g):
        v = v * lax.rsqrt(jnp.mean(v * v, axis=1, keepdims=True) + EPS) * g
        return v * cosine + pltpu.roll(v, half, 1) * sine

    loads["q_gain"].wait()
    loads["key_gain"].wait()
    loads["w_q"].wait()
    query = dot(normed, w_q[...])
    loads["w_kv"].wait()
    key_value = dot(normed, w_kv[...])
    query_gain = q_gain[...].astype(F32)
    made = [
        rotated(query[:, i * head_dim : (i + 1) * head_dim], query_gain)
        for i in range(own_heads)
    ]
    made.append(
        jnp.where(me < kv_heads, rotated(key_value, key_gain[...].astype(F32)), key_value)
    )
    made.append(jnp.zeros((LANES - (own_heads + 1) * tokens, head_dim), F32))
    made = jnp.concatenate(made, axis=0).astype(BF16)
    heads_out[...] = dot(order_out, made).astype(BF16).reshape(heads_out.shape)
    heads_in[me] = heads_out[me]
    loop(
        n_et,
        lambda i: et_copy(
            HEADS, heads_out.at[et_peer(i)], heads_in.at[me], et_peer(i)
        ).start(),
    )

    rows_of = cache_hbm.shape[0] // local
    piece = 768
    own_lane = iota((1, tokens), 1)
    lengths = length[...].astype(F32)
    loads["cache"].wait()
    loop(
        n_et,
        lambda i: et_arrival(
            HEADS, heads_out.at[et_peer(i)], heads_in.at[et_peer(i)], et_peer(i)
        ).wait_recv(),
    )
    ordered = dot(order_in, heads_in[...].reshape(n_et * pad, head_dim))
    for t in range(local):
        q = ordered[t * n_heads : (t + 1) * n_heads]
        new_key = ordered[per + t * n_heads : per + (t + 1) * n_heads]
        new_value = ordered[2 * per + t * n_heads : 2 * per + (t + 1) * n_heads]
        fresh = jnp.exp(jnp.sum(q * new_key, axis=1, keepdims=True) * scale)
        limit = (
            jnp.sum(
                jnp.where(own_lane == me * local + t, lengths, 0.0),
                axis=1,
                keepdims=True,
            )
            * float(2 * kv_heads)
        ).astype(jnp.int32)
        q = q.astype(BF16)
        column = iota((n_heads, piece), 1)
        aligned = lax.rem(column, 2 * kv_heads) == 2 * lax.div(
            iota((n_heads, piece), 0), group
        )
        total = fresh
        summed = fresh * new_value
        for p in range(rows_of // piece):
            block = cache[t * rows_of + p * piece : t * rows_of + (p + 1) * piece, :]
            score = dot_nt(q, block)
            live = aligned & (column < limit - p * piece)
            weights = jnp.where(live, jnp.exp(score * scale), 0.0)
            total = total + jnp.sum(weights, axis=1, keepdims=True)
            moved = jnp.concatenate(
                [
                    pltpu.roll(weights[:, i : i + LANES], 1, 1)
                    for i in range(0, piece, LANES)
                ],
                axis=1,
            )
            summed = summed + dot(moved.astype(BF16), block)
        mixed_out[t * n_heads : (t + 1) * n_heads, :] = (summed / total).astype(BF16)
    mixed_in[me] = mixed_out[...]
    loop(
        n_et,
        lambda i: et_copy(MIXED, mixed_out, mixed_in.at[me], et_peer(i)).start(),
    )

    loads["w_o"].wait()
    loop(
        n_et,
        lambda i: et_arrival(
            MIXED, mixed_out, mixed_in.at[et_peer(i)], et_peer(i)
        ).wait_recv(),
    )
    mixed_f[...] = mixed_in[...].reshape(tokens * n_heads, head_dim).astype(F32)
    attended = jnp.concatenate(
        [mixed_f[pl.ds(h, tokens, stride=n_heads), :] for h in range(n_heads)], axis=1
    ).astype(BF16)
    resid = (features[me].astype(F32) + dot(attended, w_o[...])).astype(BF16)

    sent = dot(placed, resid)
    sent = sent.reshape(n_stream, n_local * CAP, 2 * LANES)
    rows_out[...] = jnp.concatenate(
        [sent[:, :, :LANES], sent[:, :, LANES:]], axis=1
    ).astype(BF16)
    rows_in[me_s] = rows_out[me_s]
    loop(
        n_stream,
        lambda i: stream_copy(
            OUTWARD, rows_out.at[stream_peer(i)], rows_in.at[me_s], stream_peer(i)
        ).start(),
    )
    loads["moe_gain"].wait()
    gain = moe_gain[...].astype(F32)
    gain = jnp.concatenate([gain[0:1], gain[1:2]], axis=1)
    loads["w_gu"].wait()
    loop(
        n_stream,
        lambda i: stream_arrival(
            OUTWARD, rows_out.at[stream_peer(i)], rows_in.at[stream_peer(i)], stream_peer(i)
        ).wait_recv(),
    )
    chunk = 2 * n_local * CAP
    rows_f[...] = rows_in[...].reshape(n_stream * chunk, LANES).astype(F32)
    for j in range(n_local):
        taken = []
        for c in range(CAP):
            taken.append(
                jnp.concatenate(
                    [
                        rows_f[
                            pl.ds(h * n_local * CAP + c * n_local + j, n_stream, stride=chunk), :
                        ]
                        for h in range(2)
                    ],
                    axis=1,
                )
            )
        taken = jnp.concatenate(taken, axis=0)
        squares = jnp.sum(taken * taken, axis=1, keepdims=True)
        high = squares.astype(BF16).astype(F32)
        expert_squares[j] = jnp.where(
            iota((CAP * n_stream, LANES), 1) < LANES // 2, high, squares - high
        )
        expert_rows[j] = (taken * gain).astype(BF16)

    hidden_width = w_down_hbm.shape[1]
    for i in range(n_local):
        j = lax.rem(lax.div(me, CAP) + 1 + i, n_local)
        taken = expert_rows[j]
        products = jnp.concatenate(
            [dot(taken, w_gu[j, 0]), dot(taken, w_gu[j, 1]), expert_squares[j]], axis=1
        )
        pairs_out[i] = products.astype(BF16).reshape(pairs_out.shape[1:])
        if i < n_local - 1:
            for c in range(CAP):
                et_copy(
                    PAIRS, pairs_out.at[i, c], pairs_in.at[me], CAP * j + c
                ).start()
        else:
            pairs_own[...] = products.reshape(pairs_own.shape)
            c = 1 - lax.rem(me, CAP)
            et_copy(PAIRS, pairs_out.at[i, c], pairs_in.at[me], CAP * j + c).start()
    pair = pairs_own[lax.rem(me, CAP)]
    for i in range(1, n_et):
        et_arrival(
            PAIRS, pairs_out.at[0, 0], pairs_in.at[et_peer(i)], et_peer(i)
        ).wait_recv()
        pair = pair + pairs_in[et_peer(i)].astype(F32)
    squares = jnp.sum(pair[:, 2 * hidden_width :], axis=1, keepdims=True) * (
        2.0 / LANES / width
    )
    level = lax.rsqrt(squares + EPS)
    first = pair[:, :hidden_width] * level
    second = pair[:, hidden_width : 2 * hidden_width] * level
    hidden_out[...] = (first / (1.0 + jnp.exp(-first)) * second).astype(BF16)
    hidden_in[me] = hidden_out[...]
    loop(
        n_et,
        lambda i: et_copy(HIDDEN, hidden_out, hidden_in.at[me], et_peer(i)).start(),
    )

    loads["w_down"].wait()
    loop(
        n_et,
        lambda i: et_arrival(
            HIDDEN, hidden_out, hidden_in.at[et_peer(i)], et_peer(i)
        ).wait_recv(),
    )
    for j in range(n_local):
        hidden = hidden_in[CAP * j : CAP * (j + 1)].reshape(CAP * n_stream, hidden_width)
        result = dot(hidden, w_down[j])
        for c in range(CAP):
            for h in range(2):
                results_f[
                    pl.ds(h * n_local * CAP + c * n_local + j, n_stream, stride=chunk), :
                ] = result[c * n_stream : (c + 1) * n_stream, h * LANES : (h + 1) * LANES]
    results_out[...] = results_f[...].astype(BF16).reshape(results_out.shape)
    results_in[me_s] = results_out[me_s]
    loop(
        n_stream,
        lambda i: stream_copy(
            HOME, results_out.at[stream_peer(i)], results_in.at[me_s], stream_peer(i)
        ).start(),
    )
    loop(
        n_stream,
        lambda i: stream_arrival(
            HOME, results_out.at[stream_peer(i)], results_in.at[stream_peer(i)], stream_peer(i)
        ).wait_recv(),
    )
    returned = results_in[...].astype(F32)
    returned = (
        jnp.concatenate(
            [returned[:, : n_local * CAP], returned[:, n_local * CAP :]], axis=2
        )
        .reshape(slots, 2 * LANES)
        .astype(BF16)
    )
    routed = dot_tn(mixing_high, returned) + dot_tn(mixing_low, returned)
    out_ref[...] = (resid.astype(F32) + routed).astype(BF16)

    def sent_et(exchange, source, target):
        loop(
            n_et,
            lambda i: et_copy(exchange, source, target, et_peer(i)).wait_send(),
        )

    sent_et(FEATURES, res_hbm, features.at[me])
    sent_et(HEADS, heads_out.at[0], heads_in.at[me])
    sent_et(MIXED, mixed_out, mixed_in.at[me])
    sent_et(PAIRS, pairs_out.at[0, 0], pairs_in.at[me])
    sent_et(HIDDEN, hidden_out, hidden_in.at[me])
    for exchange, source, target in (
        (OUTWARD, rows_out, rows_in),
        (HOME, results_out, results_in),
    ):
        loop(
            n_stream,
            lambda i: stream_copy(
                exchange, source.at[stream_peer(i)], target.at[me_s], stream_peer(i)
            ).wait_send(),
        )


def on_device(
    n_stream,
    n_et,
    residual_in,
    attn_gain,
    q_gain,
    key_norm_gain,
    w_q,
    key_value_weight,
    w_o,
    key_value_cache,
    cache_length,
    moe_gain,
    route_ids,
    route_gates,
    w_gate_up,
    w_down,
):
    tokens, features = residual_in.shape
    head_dim = q_gain.shape[0]
    local, span, _, kv_width = key_value_cache.shape
    kv_heads = kv_width // head_dim
    n_heads = w_q.shape[1] // head_dim * n_et
    n_local = w_gate_up.shape[0]
    hidden = w_down.shape[1]
    cache = (
        key_value_cache.reshape(local, span, 2, kv_heads, head_dim)
        .transpose(0, 1, 3, 2, 4)
        .reshape(local * span * kv_heads * 2, head_dim)
    )
    args = (
        residual_in,
        attn_gain.reshape(-1, LANES),
        q_gain.reshape(1, -1),
        key_norm_gain.reshape(1, -1),
        w_q,
        key_value_weight,
        w_o,
        cache,
        cache_length.reshape(1, -1),
        moe_gain.reshape(-1, LANES),
        route_ids.T,
        route_gates.T,
        w_gate_up,
        w_down,
    )
    chunk = 2 * n_local * CAP
    vmem = pltpu.VMEM
    row_blocks = (n_stream, chunk, LANES)
    flat_rows = (n_stream * chunk, LANES)
    pair_width = 2 * hidden + LANES
    scratch = [vmem(a.shape, a.dtype) for a in args[1:]] + [
        vmem((n_et, tokens, features), BF16),
        vmem((n_et, 16, head_dim), BF16),
        vmem((n_et, 16, head_dim), BF16),
        vmem((local * n_heads, head_dim), BF16),
        vmem((n_et, local * n_heads, head_dim), BF16),
        vmem((tokens * n_heads, head_dim), F32),
        vmem(row_blocks, BF16),
        vmem(row_blocks, BF16),
        vmem(flat_rows, F32),
        vmem((n_local, CAP * n_stream, features), BF16),
        vmem((n_local, CAP * n_stream, LANES), F32),
        vmem((n_local, CAP, n_stream, pair_width), BF16),
        vmem((CAP, n_stream, pair_width), F32),
        vmem((n_et, n_stream, pair_width), BF16),
        vmem((n_stream, hidden), BF16),
        vmem((n_et, n_stream, hidden), BF16),
        vmem(flat_rows, F32),
        vmem(row_blocks, BF16),
        vmem(row_blocks, BF16),
        pltpu.SemaphoreType.DMA((len(args),)),
        pltpu.SemaphoreType.DMA((5, n_et)),
        pltpu.SemaphoreType.DMA((5, n_et)),
        pltpu.SemaphoreType.DMA((2, n_stream)),
        pltpu.SemaphoreType.DMA((2, n_stream)),
    ]
    return pl.pallas_call(
        functools.partial(kernel, n_stream, n_et),
        out_shape=jax.ShapeDtypeStruct(residual_in.shape, residual_in.dtype),
        in_specs=[pl.BlockSpec(memory_space=pl.ANY)] * len(args),
        out_specs=pl.BlockSpec(memory_space=pltpu.VMEM),
        scratch_shapes=scratch,
        compiler_params=pltpu.CompilerParams(
            collective_id=0, has_side_effects=True, vmem_limit_bytes=56 * 1024 * 1024
        ),
    )(*args)


def solution(mesh):
    placed = (
        P("stream", "et"),
        P(),
        P(),
        P(),
        P(None, "et"),
        P(None, "et"),
        P(None, "et"),
        P(("stream", "et"), None, None, None),
        P("stream"),
        P("et"),
        P("stream", None),
        P("stream", None),
        P("stream", None, "et", None),
        P("stream", None, "et"),
    )
    return jax.shard_map(
        functools.partial(on_device, mesh.shape["stream"], mesh.shape["et"]),
        mesh=mesh,
        in_specs=placed,
        out_specs=P("stream", "et"),
        check_vma=False,
    )
```

time: 278 us -> 72.1 us (0.26)
  blocking collectives: 122 us -> 0 us
  waiting for transfers between devices: 87.6 us -> 0 us
  Pallas kernels: 0 us -> 70.6 us
  local copies, waits for them, and re-layouts: 27.3 us -> 1.3 us
  between operations: 13.7 us -> 0.01 us
  matrix products: 12.8 us -> 0 us
  starting transfers between devices: 9.55 us -> 0 us
  other arithmetic: 4.33 us -> 0 us
    psum x1 -> x0, waiting for transfers between devices: 82.6 us -> none  [on_device(): pair = lax.psum(partial_value, 'et')]
    pallas_call x0 -> x1, Pallas kernels: none -> 70.6 us  [on_device(): pl.pallas_call(functools.partial(kernel, n_stream, n_et), out_shape=jax.S...]
    all_to_all x2 -> x0, blocking collectives: 62.9 us -> none  [the longest x1 40.5 us: on_device(): lax.all_to_all(outgoing, 'stream', split_axis=0, concat_axis=0, tiled=True)]
    all_gather x2 -> x0, blocking collectives: 45.2 us -> none  [the longest x1 23.4 us: on_device(): full_input = lax.all_gather(residual_in, 'et', axis=1, tiled=True)]
    unnamed x21 -> x1, local copies, waits for them, and re-layouts: 16.7 us -> 1.3 us
    psum x1 -> x0, blocking collectives: 13.4 us -> none  [on_device(): squares = lax.psum(jnp.sum(resid_f * resid_f, axis=-1), 'et')]
    dot_general x9 -> x0, matrix products: 12.8 us -> none  [the longest x1 2.31 us: on_device(): jnp.einsum('secf,efd->secd', hidden, w_down, preferred_element_type=jnp.f...]
    all_to_all x2 -> x0, starting transfers between devices: 9.51 us -> none  [the longest x1 5.15 us: on_device(): lax.all_to_all(own_query.reshape(input_rows, -1), 'et', split_axis=0, con...]
  transfers between devices with their start and end apart: 3 -> 0, of which waited for: 2 -> 0; matrix products, arithmetic and copies ran while one was open for 10% -> 0% of each run, Pallas kernels for 0% -> 0%
where the time goes in v1:
time: 72.1 us; the launch traced here: 71.9 us
  Pallas kernels  70.6 us (98%)
  local copies, waits for them, and re-layouts  1.3 us (2%)
    pallas_call x1, Pallas kernels, on_device(): pl.pallas_call(functools.partial(kernel, n_stream, n_et), out_shape=jax.S...  70.6 us

profile of v1, /device:TPU:1, one launch (start us, length us, event | category | flops | bytes accessed | tf_op | source)
XLA Modules:
  0.0 71.9 jit_solution(13092760544638632148)
XLA Ops:
  0.0 70.6 %shard_map.136 = bf16[16,256]{1,0:T(8,128)(2,1)} custom-call(bf16[16,256]{1,0:T(8,128)(2,1)} %res_hbm.1, bf16[16,128]{1,0:T(8,128)(2,1)} %bitcast.13, bf16[1,128]{1,0:T(2,128)(2,1)} %bitcast.16, bf16[1,128]{1,0:T(2,128)(2,1)} %bitcast.17, bf16[2048,512]{1,0:T(8,128)(2,1)} %w_q_hbm.1, bf16[2048,128]{1,0:T(8,128)(2,1)} %w_kv_hbm.1, bf16[4096,256]{1,0:T(8,128)(2,1)} %w_o_hbm.1, ...), custom_call_target="tpu_custom_call" | custom-call | tf_op jit(solution)/shard_map/pallas_call | solution.py:597
  70.6 1.3 %copy.17 = bf16[16,256]{1,0:T(8,128)(2,1)} copy(bf16[16,256]{1,0:T(8,128)(2,1)} %shard_map.136) | data formatting | bytes 16384

commit v2 on v1

--- a/solution.py
+++ b/solution.py
@@ -132,6 +132,20 @@
     def stream_peer(step):
         return lax.rem(me_s + step, n_stream)
 
+    def far_first():
+        if n_stream % 4:
+            return [stream_peer(i) for i in range(1, n_stream)]
+        deep = n_stream // 4
+        y, z, core = lax.div(me_s, 2 * deep), lax.rem(lax.div(me_s, 2), deep), lax.rem(me_s, 2)
+        away = sorted(range(deep), key=lambda i: -min(i, deep - i))
+        return [
+            lax.rem(y + dy, 2) * (2 * deep) + lax.rem(z + dz, deep) * 2 + lax.rem(core + dc, 2)
+            for dz in away
+            for dy in (1, 0)
+            for dc in (1, 0)
+            if dz or dy or dc
+        ]
+
     def et_copy(exchange, source, target, peer):
         return pltpu.make_async_remote_copy(
             src_ref=source,
@@ -307,7 +321,7 @@
     )
 
     rows_of = cache_hbm.shape[0] // local
-    piece = 768
+    piece = rows_of
     own_lane = iota((1, tokens), 1)
     lengths = length[...].astype(F32)
     loads["cache"].wait()
@@ -378,12 +392,8 @@
         [sent[:, :, :LANES], sent[:, :, LANES:]], axis=1
     ).astype(BF16)
     rows_in[me_s] = rows_out[me_s]
-    loop(
-        n_stream,
-        lambda i: stream_copy(
-            OUTWARD, rows_out.at[stream_peer(i)], rows_in.at[me_s], stream_peer(i)
-        ).start(),
-    )
+    for peer in far_first():
+        stream_copy(OUTWARD, rows_out.at[peer], rows_in.at[me_s], peer).start()
     loads["moe_gain"].wait()
     gain = moe_gain[...].astype(F32)
     gain = jnp.concatenate([gain[0:1], gain[1:2]], axis=1)
@@ -420,7 +430,7 @@
 
     hidden_width = w_down_hbm.shape[1]
     for i in range(n_local):
-        j = lax.rem(lax.div(me, CAP) + 1 + i, n_local)
+        j = lax.rem(lax.div(me, CAP) + (2, 1, 3, 0)[i], n_local)
         taken = expert_rows[j]
         products = jnp.concatenate(
             [dot(taken, w_gu[j, 0]), dot(taken, w_gu[j, 1]), expert_squares[j]], axis=1
@@ -471,12 +481,8 @@
                 ] = result[c * n_stream : (c + 1) * n_stream, h * LANES : (h + 1) * LANES]
     results_out[...] = results_f[...].astype(BF16).reshape(results_out.shape)
     results_in[me_s] = results_out[me_s]
-    loop(
-        n_stream,
-        lambda i: stream_copy(
-            HOME, results_out.at[stream_peer(i)], results_in.at[me_s], stream_peer(i)
-        ).start(),
-    )
+    for peer in far_first():
+        stream_copy(HOME, results_out.at[peer], results_in.at[me_s], peer).start()
     loop(
         n_stream,
         lambda i: stream_arrival(

time: 72.1 us -> 65.1 us (0.903)
  Pallas kernels: 70.6 us -> 63.6 us
    pallas_call x1, Pallas kernels: 70.6 us -> 63.6 us  [on_device(): pl.pallas_call(functools.partial(kernel, n_stream, n_et), out_shape=jax.S...]
where the time goes in v2:
time: 65.1 us; the launch traced here: 64.9 us
  Pallas kernels  63.6 us (98%)
  local copies, waits for them, and re-layouts  1.3 us (2%)
    pallas_call x1, Pallas kernels, on_device(): pl.pallas_call(functools.partial(kernel, n_stream, n_et), out_shape=jax.S...  63.6 us

profile of v2, /device:TPU:1, one launch (start us, length us, event | category | flops | bytes accessed | tf_op | source)
XLA Modules:
  0.0 64.9 jit_solution(9799850141549921936)
XLA Ops:
  0.0 63.6 %shard_map.136 = bf16[16,256]{1,0:T(8,128)(2,1)} custom-call(bf16[16,256]{1,0:T(8,128)(2,1)} %res_hbm.1, bf16[16,128]{1,0:T(8,128)(2,1)} %bitcast.13, bf16[1,128]{1,0:T(2,128)(2,1)} %bitcast.16, bf16[1,128]{1,0:T(2,128)(2,1)} %bitcast.17, bf16[2048,512]{1,0:T(8,128)(2,1)} %w_q_hbm.1, bf16[2048,128]{1,0:T(8,128)(2,1)} %w_kv_hbm.1, bf16[4096,256]{1,0:T(8,128)(2,1)} %w_o_hbm.1, ...), custom_call_target="tpu_custom_call" | custom-call | tf_op jit(solution)/shard_map/pallas_call | solution.py:603
  63.6 1.3 %copy.17 = bf16[16,256]{1,0:T(8,128)(2,1)} copy(bf16[16,256]{1,0:T(8,128)(2,1)} %shard_map.136) | data formatting | bytes 16384

commit v3 on v2

--- a/solution.py
+++ b/solution.py
@@ -91,6 +91,7 @@
     et_recv,
     stream_send,
     stream_recv,
+    known,
 ):
     me_s = lax.axis_index("stream")
     me = lax.axis_index("et")
@@ -105,6 +106,108 @@
     n_local = w_gu_hbm.shape[0]
     slots = n_stream * n_local * CAP
     scale = head_dim**-0.5
+
+    def et_peer(step):
+        return lax.rem(me + step, n_et)
+
+    def stream_peer(step):
+        return lax.rem(me_s + step, n_stream)
+
+    n_y, n_z, n_core = (2, n_stream // 4, 2) if n_stream % 4 == 0 else (1, 1, n_stream)
+    y, z, core = lax.div(me_s, n_z * n_core), lax.rem(lax.div(me_s, n_core), n_z), lax.rem(me_s, n_core)
+
+    def stream_at(dy, dz, dc):
+        return (
+            lax.rem(y + dy, n_y) * (n_z * n_core)
+            + lax.rem(z + dz, n_z) * n_core
+            + lax.rem(core + dc, n_core)
+        )
+
+    across = [(dy, 0, dc) for dy in range(n_y) for dc in range(n_core) if dy or dc]
+
+    def along(reach):
+        return [(0, dz, 0) for dz in sorted({reach % n_z, -reach % n_z} - {0})]
+
+    rounds = []
+    reach = 1
+    while reach < n_z // 2:
+        rounds.append(along(reach))
+        reach *= 2
+    rounds.append(across)
+
+    def tell(number):
+        for away in rounds[number] if number < len(rounds) else ():
+            pl.semaphore_signal(
+                known.at[number],
+                inc=1,
+                device_id=(stream_at(*away), me),
+                device_id_type=MESH,
+            )
+
+    def hear(number):
+        if number < len(rounds):
+            pl.semaphore_wait(known.at[number], len(rounds[number]))
+
+    far_first = [
+        stream_at(dy, dz, dc)
+        for dz in sorted(range(n_z), key=lambda i: -min(i, n_z - i))
+        for dy in reversed(range(n_y))
+        for dc in reversed(range(n_core))
+        if dy or dz or dc
+    ]
+
+    def et_copy(exchange, source, target, peer):
+        return pltpu.make_async_remote_copy(
+            src_ref=source,
+            dst_ref=target,
+            send_sem=et_send.at[exchange, peer],
+            recv_sem=et_recv.at[exchange, me],
+            device_id=(me_s, peer),
+            device_id_type=MESH,
+        )
+
+    def et_arrival(exchange, source, target, peer):
+        return pltpu.make_async_remote_copy(
+            src_ref=source,
+            dst_ref=target,
+            send_sem=et_send.at[exchange, peer],
+            recv_sem=et_recv.at[exchange, peer],
+            device_id=(me_s, peer),
+            device_id_type=MESH,
+        )
+
+    def stream_copy(exchange, source, target, peer):
+        return pltpu.make_async_remote_copy(
+            src_ref=source,
+            dst_ref=target,
+            send_sem=stream_send.at[exchange, peer],
+            recv_sem=stream_recv.at[exchange, me_s],
+            device_id=(peer, me),
+            device_id_type=MESH,
+        )
+
+    def stream_arrival(exchange, source, target, peer):
+        return pltpu.make_async_remote_copy(
+            src_ref=source,
+            dst_ref=target,
+            send_sem=stream_send.at[exchange, peer],
+            recv_sem=stream_recv.at[exchange, peer],
+            device_id=(peer, me),
+            device_id_type=MESH,
+        )
+
+    def loop(n, body):
+        def step(i, carry):
+            body(i)
+            return carry
+
+        lax.fori_loop(1, n, step, 0)
+
+    barrier = pltpu.get_barrier_semaphore()
+    greeted = [(me_s, et_peer(i)) for i in range(1, n_et)]
+    greeted += [(stream_at(*away), me) for away in along(1) + across]
+    for device in greeted:
+        pl.semaphore_signal(barrier, inc=1, device_id=device, device_id_type=MESH)
 
     loads = {}
     for name, source, target in (
@@ -126,92 +229,13 @@
         loads[name] = pltpu.make_async_copy(source, target, load_sem.at[len(loads)])
         loads[name].start()
 
-    def et_peer(step):
-        return lax.rem(me + step, n_et)
-
-    def stream_peer(step):
-        return lax.rem(me_s + step, n_stream)
-
-    def far_first():
-        if n_stream % 4:
-            return [stream_peer(i) for i in range(1, n_stream)]
-        deep = n_stream // 4
-        y, z, core = lax.div(me_s, 2 * deep), lax.rem(lax.div(me_s, 2), deep), lax.rem(me_s, 2)
-        away = sorted(range(deep), key=lambda i: -min(i, deep - i))
-        return [
-            lax.rem(y + dy, 2) * (2 * deep) + lax.rem(z + dz, deep) * 2 + lax.rem(core + dc, 2)
-            for dz in away
-            for dy in (1, 0)
-            for dc in (1, 0)
-            if dz or dy or dc
-        ]
-
-    def et_copy(exchange, source, target, peer):
-        return pltpu.make_async_remote_copy(
-            src_ref=source,
-            dst_ref=target,
-            send_sem=et_send.at[exchange, peer],
-            recv_sem=et_recv.at[exchange, me],
-            device_id=(me_s, peer),
-            device_id_type=MESH,
-        )
-
-    def et_arrival(exchange, source, target, peer):
-        return pltpu.make_async_remote_copy(
-            src_ref=source,
-            dst_ref=target,
-            send_sem=et_send.at[exchange, peer],
-            recv_sem=et_recv.at[exchange, peer],
-            device_id=(me_s, peer),
-            device_id_type=MESH,
-        )
-
-    def stream_copy(exchange, source, target, peer):
-        return pltpu.make_async_remote_copy(
-            src_ref=source,
-            dst_ref=target,
-            send_sem=stream_send.at[exchange, peer],
-            recv_sem=stream_recv.at[exchange, me_s],
-            device_id=(peer, me),
-            device_id_type=MESH,
-        )
-
-    def stream_arrival(exchange, source, target, peer):
-        return pltpu.make_async_remote_copy(
-            src_ref=source,
-            dst_ref=target,
-            send_sem=stream_send.at[exchange, peer],
-            recv_sem=stream_recv.at[exchange, peer],
-            device_id=(peer, me),
-            device_id_type=MESH,
-        )
-
-    def loop(n, body):
-        def step(i, carry):
-            body(i)
-            return carry
-
-        lax.fori_loop(1, n, step, 0)
-
-    barrier = pltpu.get_barrier_semaphore()
-    loop(
-        n_et,
-        lambda i: pl.semaphore_signal(
-            barrier, inc=1, device_id=(me_s, et_peer(i)), device_id_type=MESH
-        ),
-    )
-    loop(
-        n_stream,
-        lambda i: pl.semaphore_signal(
-            barrier, inc=1, device_id=(stream_peer(i), me), device_id_type=MESH
-        ),
-    )
-    pl.semaphore_wait(barrier, n_et + n_stream - 2)
+    pl.semaphore_wait(barrier, len(greeted))
 
     loop(
         n_et,
         lambda i: et_copy(FEATURES, res_hbm, features.at[me], et_peer(i)).start(),
     )
+    tell(0)
 
     loads["length"].wait()
     lengths = jnp.broadcast_to(length[...], (tokens, tokens)).astype(F32)
@@ -319,6 +343,8 @@
             HEADS, heads_out.at[et_peer(i)], heads_in.at[me], et_peer(i)
         ).start(),
     )
+    hear(0)
+    tell(1)
 
     rows_of = cache_hbm.shape[0] // local
     piece = rows_of
@@ -372,6 +398,8 @@
         n_et,
         lambda i: et_copy(MIXED, mixed_out, mixed_in.at[me], et_peer(i)).start(),
     )
+    hear(1)
+    tell(2)
 
     loads["w_o"].wait()
     loop(
@@ -392,7 +420,8 @@
         [sent[:, :, :LANES], sent[:, :, LANES:]], axis=1
     ).astype(BF16)
     rows_in[me_s] = rows_out[me_s]
-    for peer in far_first():
+    hear(2)
+    for peer in far_first:
         stream_copy(OUTWARD, rows_out.at[peer], rows_in.at[me_s], peer).start()
     loads["moe_gain"].wait()
     gain = moe_gain[...].astype(F32)
@@ -481,7 +510,7 @@
                 ] = result[c * n_stream : (c + 1) * n_stream, h * LANES : (h + 1) * LANES]
     results_out[...] = results_f[...].astype(BF16).reshape(results_out.shape)
     results_in[me_s] = results_out[me_s]
-    for peer in far_first():
+    for peer in far_first:
         stream_copy(HOME, results_out.at[peer], results_in.at[me_s], peer).start()
     loop(
         n_stream,
@@ -599,6 +628,7 @@
         pltpu.SemaphoreType.DMA((5, n_et)),
         pltpu.SemaphoreType.DMA((2, n_stream)),
         pltpu.SemaphoreType.DMA((2, n_stream)),
+        pltpu.SemaphoreType.REGULAR((3,)),
     ]
     return pl.pallas_call(
         functools.partial(kernel, n_stream, n_et),

time: 65.1 us -> 62.4 us (0.959)
  Pallas kernels: 63.6 us -> 60.9 us
    pallas_call x1, Pallas kernels: 63.6 us -> 60.9 us  [on_device(): pl.pallas_call(functools.partial(kernel, n_stream, n_et), out_shape=jax.S...]
where the time goes in v3:
time: 62.4 us; the launch traced here: 62.2 us
  Pallas kernels  60.9 us (98%)
  local copies, waits for them, and re-layouts  1.3 us (2%)
    pallas_call x1, Pallas kernels, on_device(): pl.pallas_call(functools.partial(kernel, n_stream, n_et), out_shape=jax.S...  60.9 us
    unnamed x1, local copies, waits for them, and re-layouts  1.3 us

profile of v3, /device:TPU:1, one launch (start us, length us, event | category | flops | bytes accessed | tf_op | source)
XLA Modules:
  0.0 62.2 jit_solution(8256479146064949414)
XLA Ops:
  0.0 60.9 %shard_map.136 = bf16[16,256]{1,0:T(8,128)(2,1)} custom-call(bf16[16,256]{1,0:T(8,128)(2,1)} %res_hbm.1, bf16[16,128]{1,0:T(8,128)(2,1)} %bitcast.13, bf16[1,128]{1,0:T(2,128)(2,1)} %bitcast.16, bf16[1,128]{1,0:T(2,128)(2,1)} %bitcast.17, bf16[2048,512]{1,0:T(8,128)(2,1)} %w_q_hbm.1, bf16[2048,128]{1,0:T(8,128)(2,1)} %w_kv_hbm.1, bf16[4096,256]{1,0:T(8,128)(2,1)} %w_o_hbm.1, ...), custom_call_target="tpu_custom_call" | custom-call | tf_op jit(solution)/shard_map/pallas_call | solution.py:633
  60.9 1.3 %copy.17 = bf16[16,256]{1,0:T(8,128)(2,1)} copy(bf16[16,256]{1,0:T(8,128)(2,1)} %shard_map.136) | data formatting | bytes 16384

commit v4 on v3

--- a/solution.py
+++ b/solution.py
@@ -156,6 +156,15 @@
         if dy or dz or dc
     ]
 
+    n_x = n_et // 2
+    x, y_low = lax.div(me, 2), lax.rem(me, 2)
+    et_far_first = [
+        lax.rem(x + dx, n_x) * 2 + lax.rem(y_low + dy, 2)
+        for dx in sorted(range(n_x), key=lambda i: -min(i, n_x - i))
+        for dy in (1, 0)
+        if dx or dy
+    ]
+
     def et_copy(exchange, source, target, peer):
         return pltpu.make_async_remote_copy(
             src_ref=source,
@@ -204,10 +213,16 @@
         lax.fori_loop(1, n, step, 0)
 
     barrier = pltpu.get_barrier_semaphore()
-    greeted = [(me_s, et_peer(i)) for i in range(1, n_et)]
+    greeted = [(me_s, peer) for peer in et_far_first]
     greeted += [(stream_at(*away), me) for away in along(1) + across]
     for device in greeted:
         pl.semaphore_signal(barrier, inc=1, device_id=device, device_id_type=MESH)
+
+    pl.semaphore_wait(barrier, len(greeted))
+
+    for peer in et_far_first:
+        et_copy(FEATURES, res_hbm, features.at[me], peer).start()
+    tell(0)
 
     loads = {}
     for name, source, target in (
@@ -228,14 +243,6 @@
     ):
         loads[name] = pltpu.make_async_copy(source, target, load_sem.at[len(loads)])
         loads[name].start()
-
-    pl.semaphore_wait(barrier, len(greeted))
-
-    loop(
-        n_et,
-        lambda i: et_copy(FEATURES, res_hbm, features.at[me], et_peer(i)).start(),
-    )
-    tell(0)
 
     loads["length"].wait()
     lengths = jnp.broadcast_to(length[...], (tokens, tokens)).astype(F32)
@@ -337,12 +344,8 @@
     made = jnp.concatenate(made, axis=0).astype(BF16)
     heads_out[...] = dot(order_out, made).astype(BF16).reshape(heads_out.shape)
     heads_in[me] = heads_out[me]
-    loop(
-        n_et,
-        lambda i: et_copy(
-            HEADS, heads_out.at[et_peer(i)], heads_in.at[me], et_peer(i)
-        ).start(),
-    )
+    for peer in et_far_first:
+        et_copy(HEADS, heads_out.at[peer], heads_in.at[me], peer).start()
     hear(0)
     tell(1)
 
@@ -394,10 +397,8 @@
             summed = summed + dot(moved.astype(BF16), block)
         mixed_out[t * n_heads : (t + 1) * n_heads, :] = (summed / total).astype(BF16)
     mixed_in[me] = mixed_out[...]
-    loop(
-        n_et,
-        lambda i: et_copy(MIXED, mixed_out, mixed_in.at[me], et_peer(i)).start(),
-    )
+    for peer in et_far_first:
+        et_copy(MIXED, mixed_out, mixed_in.at[me], peer).start()
     hear(1)
     tell(2)
 
@@ -488,10 +489,8 @@
     second = pair[:, hidden_width : 2 * hidden_width] * level
     hidden_out[...] = (first / (1.0 + jnp.exp(-first)) * second).astype(BF16)
     hidden_in[me] = hidden_out[...]
-    loop(
-        n_et,
-        lambda i: et_copy(HIDDEN, hidden_out, hidden_in.at[me], et_peer(i)).start(),
-    )
+    for peer in et_far_first:
+        et_copy(HIDDEN, hidden_out, hidden_in.at[me], peer).start()
 
     loads["w_down"].wait()
     loop(
@@ -632,7 +631,7 @@
     ]
     return pl.pallas_call(
         functools.partial(kernel, n_stream, n_et),
-        out_shape=jax.ShapeDtypeStruct(residual_in.shape, residual_in.dtype),
+        out_shape=pltpu.VMEM(residual_in.shape, residual_in.dtype),
         in_specs=[pl.BlockSpec(memory_space=pl.ANY)] * len(args),
         out_specs=pl.BlockSpec(memory_space=pltpu.VMEM),
         scratch_shapes=scratch,

time: 62.4 us -> 60.4 us (0.968)
  Pallas kernels: 60.9 us -> 59.7 us
  local copies, waits for them, and re-layouts: 1.3 us -> 0.6 us
    pallas_call x1, Pallas kernels: 60.9 us -> 59.7 us  [on_device(): pl.pallas_call(functools.partial(kernel, n_stream, n_et), out_shape=pltpu...]
    unnamed x1, local copies, waits for them, and re-layouts: 1.3 us -> 0.6 us
where the time goes in v4:
time: 60.4 us; the launch traced here: 60.3 us
  Pallas kernels  59.7 us (99%)
    pallas_call x1, Pallas kernels, on_device(): pl.pallas_call(functools.partial(kernel, n_stream, n_et), out_shape=pltpu...  59.7 us

profile of v4, /device:TPU:1, one launch (start us, length us, event | category | flops | bytes accessed | tf_op | source)
XLA Modules:
  0.0 60.3 jit_solution(13553644222249631774)
XLA Ops:
  0.0 59.7 %shard_map.136 = bf16[16,256]{1,0:T(8,128)(2,1)S(1)} custom-call(bf16[16,256]{1,0:T(8,128)(2,1)} %res_hbm.1, bf16[16,128]{1,0:T(8,128)(2,1)} %bitcast.13, bf16[1,128]{1,0:T(2,128)(2,1)} %bitcast.16, bf16[1,128]{1,0:T(2,128)(2,1)} %bitcast.17, bf16[2048,512]{1,0:T(8,128)(2,1)} %w_q_hbm.1, bf16[2048,128]{1,0:T(8,128)(2,1)} %w_kv_hbm.1, ...), custom_call_target="tpu_custom_call" | custom-call | tf_op jit(solution)/shard_map/pallas_call | solution.py:632
  59.7 0.6 copy.17

commit v5 on v4

--- a/solution.py
+++ b/solution.py
@@ -16,8 +16,9 @@
 F32 = jnp.float32
 BF16 = jnp.bfloat16
 
-FEATURES, HEADS, MIXED, PAIRS, HIDDEN = range(5)
+FEATURES, HEADS, MIXED, PAIRS, HIDDEN = 0, 1, 2, 3, 5
 OUTWARD, HOME = range(2)
+WAVES = 2
 
 
 def iota(shape, dim):
@@ -148,13 +149,23 @@
         if number < len(rounds):
             pl.semaphore_wait(known.at[number], len(rounds[number]))
 
-    far_first = [
-        stream_at(dy, dz, dc)
-        for dz in sorted(range(n_z), key=lambda i: -min(i, n_z - i))
-        for dy in reversed(range(n_y))
-        for dc in reversed(range(n_core))
-        if dy or dz or dc
+    def hops(away):
+        return min(away[1], n_z - away[1]) + 2 * away[0]
+
+    def back(away):
+        return (-away[0] % n_y, -away[1] % n_z, -away[2] % n_core)
+
+    relative = sorted(
+        [(dy, dz, dc) for dy in range(n_y) for dz in range(n_z) for dc in range(n_core)],
+        key=lambda away: (hops(away), away != (0, 0, 0)),
+    )
+    share = n_stream // WAVES
+    waves = [
+        sorted(relative[w * share : (w + 1) * share], key=lambda away: -hops(away))
+        for w in range(WAVES)
     ]
+    slot_of = {away: i for i, away in enumerate(waves[0] + waves[1])}
+    at_home = slot_of[0, 0, 0]
 
     n_x = n_et // 2
     x, y_low = lax.div(me, 2), lax.rem(me, 2)
@@ -185,25 +196,28 @@
             device_id_type=MESH,
         )
 
-    def stream_copy(exchange, source, target, peer):
+    def stream_copy(exchange, source, target, away):
         return pltpu.make_async_remote_copy(
             src_ref=source,
             dst_ref=target,
-            send_sem=stream_send.at[exchange, peer],
-            recv_sem=stream_recv.at[exchange, me_s],
-            device_id=(peer, me),
+            send_sem=stream_send.at[exchange, slot_of[away]],
+            recv_sem=stream_recv.at[exchange, slot_of[back(away)]],
+            device_id=(stream_at(*away), me),
             device_id_type=MESH,
         )
 
-    def stream_arrival(exchange, source, target, peer):
+    def stream_arrival(exchange, source, target, away):
         return pltpu.make_async_remote_copy(
             src_ref=source,
             dst_ref=target,
-            send_sem=stream_send.at[exchange, peer],
-            recv_sem=stream_recv.at[exchange, peer],
-            device_id=(peer, me),
+            send_sem=stream_send.at[exchange, slot_of[away]],
+            recv_sem=stream_recv.at[exchange, slot_of[away]],
+            device_id=(stream_at(*away), me),
             device_id_type=MESH,
         )
+
+    def others(wave):
+        return [away for away in waves[wave] if away != (0, 0, 0)]
 
     def loop(n, body):
         def step(i, carry):
@@ -420,103 +434,119 @@
     rows_out[...] = jnp.concatenate(
         [sent[:, :, :LANES], sent[:, :, LANES:]], axis=1
     ).astype(BF16)
-    rows_in[me_s] = rows_out[me_s]
+    rows_in[at_home] = rows_out[me_s]
     hear(2)
-    for peer in far_first:
-        stream_copy(OUTWARD, rows_out.at[peer], rows_in.at[me_s], peer).start()
+    for w in range(WAVES):
+        for away in others(w):
+            stream_copy(
+                OUTWARD,
+                rows_out.at[stream_at(*away)],
+                rows_in.at[slot_of[back(away)]],
+                away,
+            ).start()
     loads["moe_gain"].wait()
     gain = moe_gain[...].astype(F32)
     gain = jnp.concatenate([gain[0:1], gain[1:2]], axis=1)
     loads["w_gu"].wait()
-    loop(
-        n_stream,
-        lambda i: stream_arrival(
-            OUTWARD, rows_out.at[stream_peer(i)], rows_in.at[stream_peer(i)], stream_peer(i)
-        ).wait_recv(),
-    )
     chunk = 2 * n_local * CAP
-    rows_f[...] = rows_in[...].reshape(n_stream * chunk, LANES).astype(F32)
-    for j in range(n_local):
-        taken = []
-        for c in range(CAP):
-            taken.append(
-                jnp.concatenate(
-                    [
-                        rows_f[
-                            pl.ds(h * n_local * CAP + c * n_local + j, n_stream, stride=chunk), :
-                        ]
-                        for h in range(2)
-                    ],
-                    axis=1,
+    hidden_width = w_down_hbm.shape[1]
+
+    for w in range(WAVES):
+        for away in others(w):
+            stream_arrival(
+                OUTWARD, rows_out.at[0], rows_in.at[slot_of[away]], away
+            ).wait_recv()
+        rows_f[w * share * chunk : (w + 1) * share * chunk, :] = (
+            rows_in[w * share : (w + 1) * share].reshape(share * chunk, LANES).astype(F32)
+        )
+        for j in range(n_local):
+            taken = []
+            for c in range(CAP):
+                first = w * share * chunk + c * n_local + j
+                taken.append(
+                    jnp.concatenate(
+                        [
+                            rows_f[pl.ds(first + h * n_local * CAP, share, stride=chunk), :]
+                            for h in range(2)
+                        ],
+                        axis=1,
+                    )
                 )
+            taken = jnp.concatenate(taken, axis=0)
+            squares = jnp.sum(taken * taken, axis=1, keepdims=True)
+            high = squares.astype(BF16).astype(F32)
+            expert_squares[w, j] = jnp.where(
+                iota((CAP * share, LANES), 1) < LANES // 2, high, squares - high
             )
-        taken = jnp.concatenate(taken, axis=0)
-        squares = jnp.sum(taken * taken, axis=1, keepdims=True)
-        high = squares.astype(BF16).astype(F32)
-        expert_squares[j] = jnp.where(
-            iota((CAP * n_stream, LANES), 1) < LANES // 2, high, squares - high
-        )
-        expert_rows[j] = (taken * gain).astype(BF16)
-
-    hidden_width = w_down_hbm.shape[1]
-    for i in range(n_local):
-        j = lax.rem(lax.div(me, CAP) + (2, 1, 3, 0)[i], n_local)
-        taken = expert_rows[j]
-        products = jnp.concatenate(
-            [dot(taken, w_gu[j, 0]), dot(taken, w_gu[j, 1]), expert_squares[j]], axis=1
-        )
-        pairs_out[i] = products.astype(BF16).reshape(pairs_out.shape[1:])
-        if i < n_local - 1:
+            expert_rows[w, j] = (taken * gain).astype(BF16)
+        for i in range(n_local):
+            j = lax.rem(lax.div(me, CAP) + (2, 1, 3, 0)[i], n_local)
+            taken = expert_rows[w, j]
+            products = jnp.concatenate(
+                [dot(taken, w_gu[j, 0]), dot(taken, w_gu[j, 1]), expert_squares[w, j]], axis=1
+            )
+            pairs_out[w, i] = products.astype(BF16).reshape(pairs_out.shape[2:])
+            if i < n_local - 1:
+                for c in range(CAP):
+                    et_copy(
+                        PAIRS + w, pairs_out.at[w, i, c], pairs_in.at[w, me], CAP * j + c
+                    ).start()
+            else:
+                pairs_own[w] = products.reshape(pairs_own.shape[1:])
+                c = 1 - lax.rem(me, CAP)
+                et_copy(
+                    PAIRS + w, pairs_out.at[w, i, c], pairs_in.at[w, me], CAP * j + c
+                ).start()
+    for w in range(WAVES):
+        pair = pairs_own[w, lax.rem(me, CAP)]
+        for i in range(1, n_et):
+            et_arrival(
+                PAIRS + w, pairs_out.at[w, 0, 0], pairs_in.at[w, et_peer(i)], et_peer(i)
+            ).wait_recv()
+            pair = pair + pairs_in[w, et_peer(i)].astype(F32)
+        squares = jnp.sum(pair[:, 2 * hidden_width :], axis=1, keepdims=True) * (
+            2.0 / LANES / width
+        )
+        level = lax.rsqrt(squares + EPS)
+        first = pair[:, :hidden_width] * level
+        second = pair[:, hidden_width : 2 * hidden_width] * level
+        hidden_out[w] = (first / (1.0 + jnp.exp(-first)) * second).astype(BF16)
+        for peer in et_far_first:
+            et_copy(HIDDEN + w, hidden_out.at[w], hidden_in.at[w, me], peer).start()
+        hidden_in[w, me] = hidden_out[w]
+
+    loads["w_down"].wait()
+    for w in range(WAVES):
+        loop(
+            n_et,
+            lambda i: et_arrival(
+                HIDDEN + w, hidden_out.at[w], hidden_in.at[w, et_peer(i)], et_peer(i)
+            ).wait_recv(),
+        )
+        for j in range(n_local):
+            hidden = hidden_in[w, CAP * j : CAP * (j + 1)].reshape(CAP * share, hidden_width)
+            result = dot(hidden, w_down[j])
             for c in range(CAP):
-                et_copy(
-                    PAIRS, pairs_out.at[i, c], pairs_in.at[me], CAP * j + c
-                ).start()
-        else:
-            pairs_own[...] = products.reshape(pairs_own.shape)
-            c = 1 - lax.rem(me, CAP)
-            et_copy(PAIRS, pairs_out.at[i, c], pairs_in.at[me], CAP * j + c).start()
-    pair = pairs_own[lax.rem(me, CAP)]
-    for i in range(1, n_et):
-        et_arrival(
-            PAIRS, pairs_out.at[0, 0], pairs_in.at[et_peer(i)], et_peer(i)
-        ).wait_recv()
-        pair = pair + pairs_in[et_peer(i)].astype(F32)
-    squares = jnp.sum(pair[:, 2 * hidden_width :], axis=1, keepdims=True) * (
-        2.0 / LANES / width
-    )
-    level = lax.rsqrt(squares + EPS)
-    first = pair[:, :hidden_width] * level
-    second = pair[:, hidden_width : 2 * hidden_width] * level
-    hidden_out[...] = (first / (1.0 + jnp.exp(-first)) * second).astype(BF16)
-    hidden_in[me] = hidden_out[...]
-    for peer in et_far_first:
-        et_copy(HIDDEN, hidden_out, hidden_in.at[me], peer).start()
-
-    loads["w_down"].wait()
-    loop(
-        n_et,
-        lambda i: et_arrival(
-            HIDDEN, hidden_out, hidden_in.at[et_peer(i)], et_peer(i)
-        ).wait_recv(),
-    )
-    for j in range(n_local):
-        hidden = hidden_in[CAP * j : CAP * (j + 1)].reshape(CAP * n_stream, hidden_width)
-        result = dot(hidden, w_down[j])
-        for c in range(CAP):
-            for h in range(2):
-                results_f[
-                    pl.ds(h * n_local * CAP + c * n_local + j, n_stream, stride=chunk), :
-                ] = result[c * n_stream : (c + 1) * n_stream, h * LANES : (h + 1) * LANES]
-    results_out[...] = results_f[...].astype(BF16).reshape(results_out.shape)
-    results_in[me_s] = results_out[me_s]
-    for peer in far_first:
-        stream_copy(HOME, results_out.at[peer], results_in.at[me_s], peer).start()
-    loop(
-        n_stream,
-        lambda i: stream_arrival(
-            HOME, results_out.at[stream_peer(i)], results_in.at[stream_peer(i)], stream_peer(i)
-        ).wait_recv(),
-    )
+                for h in range(2):
+                    first = w * share * chunk + h * n_local * CAP + c * n_local + j
+                    results_f[pl.ds(first, share, stride=chunk), :] = result[
+                        c * share : (c + 1) * share, h * LANES : (h + 1) * LANES
+                    ]
+        results_out[w * share : (w + 1) * share] = (
+            results_f[w * share * chunk : (w + 1) * share * chunk, :]
+            .astype(BF16)
+            .reshape(share, chunk, LANES)
+        )
+        for away in others(w):
+            stream_copy(
+                HOME, results_out.at[slot_of[away]], results_in.at[me_s], away
+            ).start()
+    results_in[me_s] = results_out[at_home]
+    for w in range(WAVES):
+        for away in others(w):
+            stream_arrival(
+                HOME, results_out.at[0], results_in.at[stream_at(*away)], away
+            ).wait_recv()
     returned = results_in[...].astype(F32)
     returned = (
         jnp.concatenate(
@@ -537,18 +567,12 @@
     sent_et(FEATURES, res_hbm, features.at[me])
     sent_et(HEADS, heads_out.at[0], heads_in.at[me])
     sent_et(MIXED, mixed_out, mixed_in.at[me])
-    sent_et(PAIRS, pairs_out.at[0, 0], pairs_in.at[me])
-    sent_et(HIDDEN, hidden_out, hidden_in.at[me])
-    for exchange, source, target in (
-        (OUTWARD, rows_out, rows_in),
-        (HOME, results_out, results_in),
-    ):
-        loop(
-            n_stream,
-            lambda i: stream_copy(
-                exchange, source.at[stream_peer(i)], target.at[me_s], stream_peer(i)
-            ).wait_send(),
-        )
+    for w in range(WAVES):
+        sent_et(PAIRS + w, pairs_out.at[w, 0, 0], pairs_in.at[w, me])
+        sent_et(HIDDEN + w, hidden_out.at[w], hidden_in.at[w, me])
+        for away in others(w):
+            stream_copy(OUTWARD, rows_out.at[0], rows_in.at[0], away).wait_send()
+            stream_copy(HOME, results_out.at[0], results_in.at[0], away).wait_send()
 
 
 def on_device(
@@ -602,6 +626,7 @@
     row_blocks = (n_stream, chunk, LANES)
     flat_rows = (n_stream * chunk, LANES)
     pair_width = 2 * hidden + LANES
+    share = n_stream // WAVES
     scratch = [vmem(a.shape, a.dtype) for a in args[1:]] + [
         vmem((n_et, tokens, features), BF16),
         vmem((n_et, 16, head_dim), BF16),
@@ -612,19 +637,19 @@
         vmem(row_blocks, BF16),
         vmem(row_blocks, BF16),
         vmem(flat_rows, F32),
-        vmem((n_local, CAP * n_stream, features), BF16),
-        vmem((n_local, CAP * n_stream, LANES), F32),
-        vmem((n_local, CAP, n_stream, pair_width), BF16),
-        vmem((CAP, n_stream, pair_width), F32),
-        vmem((n_et, n_stream, pair_width), BF16),
-        vmem((n_stream, hidden), BF16),
-        vmem((n_et, n_stream, hidden), BF16),
+        vmem((WAVES, n_local, CAP * share, features), BF16),
+        vmem((WAVES, n_local, CAP * share, LANES), F32),
+        vmem((WAVES, n_local, CAP, share, pair_width), BF16),
+        vmem((WAVES, CAP, share, pair_width), F32),
+        vmem((WAVES, n_et, share, pair_width), BF16),
+        vmem((WAVES, share, hidden), BF16),
+        vmem((WAVES, n_et, share, hidden), BF16),
         vmem(flat_rows, F32),
         vmem(row_blocks, BF16),
         vmem(row_blocks, BF16),
         pltpu.SemaphoreType.DMA((len(args),)),
-        pltpu.SemaphoreType.DMA((5, n_et)),
-        pltpu.SemaphoreType.DMA((5, n_et)),
+        pltpu.SemaphoreType.DMA((7, n_et)),
+        pltpu.SemaphoreType.DMA((7, n_et)),
         pltpu.SemaphoreType.DMA((2, n_stream)),
         pltpu.SemaphoreType.DMA((2, n_stream)),
         pltpu.SemaphoreType.REGULAR((3,)),

time: 60.4 us -> 57.6 us (0.954)
  Pallas kernels: 59.7 us -> 56.9 us
    pallas_call x1, Pallas kernels: 59.7 us -> 56.9 us  [on_device(): pl.pallas_call(functools.partial(kernel, n_stream, n_et), out_shape=pltpu...]
where the time goes in v5:
time: 57.6 us; the launch traced here: 57.5 us
  Pallas kernels  56.9 us (99%)
  local copies, waits for them, and re-layouts  0.6 us (1%)
    pallas_call x1, Pallas kernels, on_device(): pl.pallas_call(functools.partial(kernel, n_stream, n_et), out_shape=pltpu...  56.9 us

profile of v5, /device:TPU:1, one launch (start us, length us, event | category | flops | bytes accessed | tf_op | source)
XLA Modules:
  0.0 57.5 jit_solution(18052975400109406960)
XLA Ops:
  0.0 56.9 %shard_map.136 = bf16[16,256]{1,0:T(8,128)(2,1)S(1)} custom-call(bf16[16,256]{1,0:T(8,128)(2,1)} %res_hbm.1, bf16[16,128]{1,0:T(8,128)(2,1)} %bitcast.13, bf16[1,128]{1,0:T(2,128)(2,1)} %bitcast.16, bf16[1,128]{1,0:T(2,128)(2,1)} %bitcast.17, bf16[2048,512]{1,0:T(8,128)(2,1)} %w_q_hbm.1, bf16[2048,128]{1,0:T(8,128)(2,1)} %w_kv_hbm.1, ...), custom_call_target="tpu_custom_call" | custom-call | tf_op jit(solution)/shard_map/pallas_call | solution.py:657
  56.9 0.6 %copy.17 = bf16[16,256]{1,0:T(8,128)(2,1)} copy(bf16[16,256]{1,0:T(8,128)(2,1)S(1)} %shard_map.136) | data formatting | bytes 16384

commit v6 on v5

--- a/solution.py
+++ b/solution.py
@@ -68,6 +68,8 @@
     gates,
     w_gu,
     w_down,
+    cache_f,
+    split,
     features,
     heads_out,
     heads_in,
@@ -239,24 +241,22 @@
     tell(0)
 
     loads = {}
-    for name, source, target in (
-        ("own", res_hbm, features.at[me]),
-        ("length", length_hbm, length),
-        ("attn_gain", attn_gain_hbm, attn_gain),
-        ("q_gain", q_gain_hbm, q_gain),
-        ("key_gain", key_gain_hbm, key_gain),
-        ("ids", ids_hbm, ids),
-        ("gates", gates_hbm, gates),
-        ("moe_gain", moe_gain_hbm, moe_gain),
-        ("w_q", w_q_hbm, w_q),
-        ("w_kv", w_kv_hbm, w_kv),
-        ("cache", cache_hbm, cache),
-        ("w_o", w_o_hbm, w_o),
-        ("w_gu", w_gu_hbm, w_gu),
-        ("w_down", w_down_hbm, w_down),
-    ):
+
+    def load(name, source, target):
         loads[name] = pltpu.make_async_copy(source, target, load_sem.at[len(loads)])
         loads[name].start()
+
+    load("own", res_hbm, features.at[me])
+    load("length", length_hbm, length)
+    load("cache", cache_hbm, cache)
+    load("w_q", w_q_hbm, w_q)
+    load("w_kv", w_kv_hbm, w_kv)
+    load("attn_gain", attn_gain_hbm, attn_gain)
+    load("q_gain", q_gain_hbm, q_gain)
+    load("key_gain", key_gain_hbm, key_gain)
+    load("ids", ids_hbm, ids)
+    load("gates", gates_hbm, gates)
+    load("moe_gain", moe_gain_hbm, moe_gain)
 
     loads["length"].wait()
     lengths = jnp.broadcast_to(length[...], (tokens, tokens)).astype(F32)
@@ -319,6 +319,17 @@
     mixing_high = mixing.astype(BF16)
     mixing_low = (mixing - mixing_high.astype(F32)).astype(BF16)
 
+    loads["cache"].wait()
+    rows_of = cache_hbm.shape[0] // local
+    span = rows_of // (2 * kv_heads)
+    for t in range(local):
+        cache_f[...] = cache[t * rows_of : (t + 1) * rows_of, :].astype(F32)
+        for kind in range(2):
+            for h in range(kv_heads):
+                split[t, kind, h // 2, :, h % 2 * head_dim : (h % 2 + 1) * head_dim] = cache_f[
+                    pl.ds(2 * h + kind, span, stride=2 * kv_heads), :
+                ].astype(BF16)
+
     loads["own"].wait()
     loads["attn_gain"].wait()
     loop(
@@ -362,12 +373,21 @@
         et_copy(HEADS, heads_out.at[peer], heads_in.at[me], peer).start()
     hear(0)
     tell(1)
-
-    rows_of = cache_hbm.shape[0] // local
-    piece = rows_of
+    load("w_o", w_o_hbm, w_o)
+    load("w_gu", w_gu_hbm, w_gu)
+    load("w_down", w_down_hbm, w_down)
+
     own_lane = iota((1, tokens), 1)
     lengths = length[...].astype(F32)
-    loads["cache"].wait()
+    pairs = kv_heads // 2
+    column = iota((2 * group, span), 1)
+    live = []
+    for t in range(local):
+        limit = jnp.sum(
+            jnp.where(own_lane == me * local + t, lengths, 0.0), axis=1, keepdims=True
+        ).astype(jnp.int32)
+        live.append(column < limit)
+    empty = jnp.zeros((group, head_dim), F32)
     loop(
         n_et,
         lambda i: et_arrival(
@@ -375,41 +395,37 @@
         ).wait_recv(),
     )
     ordered = dot(order_in, heads_in[...].reshape(n_et * pad, head_dim))
-    for t in range(local):
-        q = ordered[t * n_heads : (t + 1) * n_heads]
-        new_key = ordered[per + t * n_heads : per + (t + 1) * n_heads]
-        new_value = ordered[2 * per + t * n_heads : 2 * per + (t + 1) * n_heads]
-        fresh = jnp.exp(jnp.sum(q * new_key, axis=1, keepdims=True) * scale)
-        limit = (
-            jnp.sum(
-                jnp.where(own_lane == me * local + t, lengths, 0.0),
-                axis=1,
-                keepdims=True,
-            )
-            * float(2 * kv_heads)
-        ).astype(jnp.int32)
-        q = q.astype(BF16)
-        column = iota((n_heads, piece), 1)
-        aligned = lax.rem(column, 2 * kv_heads) == 2 * lax.div(
-            iota((n_heads, piece), 0), group
-        )
-        total = fresh
-        summed = fresh * new_value
-        for p in range(rows_of // piece):
-            block = cache[t * rows_of + p * piece : t * rows_of + (p + 1) * piece, :]
-            score = dot_nt(q, block)
-            live = aligned & (column < limit - p * piece)
-            weights = jnp.where(live, jnp.exp(score * scale), 0.0)
-            total = total + jnp.sum(weights, axis=1, keepdims=True)
-            moved = jnp.concatenate(
-                [
-                    pltpu.roll(weights[:, i : i + LANES], 1, 1)
-                    for i in range(0, piece, LANES)
-                ],
-                axis=1,
-            )
-            summed = summed + dot(moved.astype(BF16), block)
-        mixed_out[t * n_heads : (t + 1) * n_heads, :] = (summed / total).astype(BF16)
+    q = ordered[:per]
+    blocks = []
+    for i in range(local * pairs):
+        at = i * 2 * group
+        upper = jnp.concatenate([q[at : at + group], empty], axis=1)
+        lower = jnp.concatenate([empty, q[at + group : at + 2 * group]], axis=1)
+        blocks.append(jnp.concatenate([upper, lower], axis=0).astype(BF16))
+    scores = [
+        dot_nt(block, split[i // pairs, 0, i % pairs]) for i, block in enumerate(blocks)
+    ]
+    weights = [
+        jnp.where(live[i // pairs], jnp.exp(score * scale), 0.0)
+        for i, score in enumerate(scores)
+    ]
+    summed = [
+        dot(weight.astype(BF16), split[i // pairs, 1, i % pairs])
+        for i, weight in enumerate(weights)
+    ]
+    fresh = jnp.exp(jnp.sum(q * ordered[per : 2 * per], axis=1, keepdims=True) * scale)
+    total = fresh + jnp.concatenate(
+        [jnp.sum(weight, axis=1, keepdims=True) for weight in weights], axis=0
+    )
+    summed = jnp.concatenate(
+        [
+            part
+            for both in summed
+            for part in (both[:group, :head_dim], both[group:, head_dim:])
+        ],
+        axis=0,
+    )
+    mixed_out[...] = ((summed + fresh * ordered[2 * per :]) / total).astype(BF16)
     mixed_in[me] = mixed_out[...]
     for peer in et_far_first:
         et_copy(MIXED, mixed_out, mixed_in.at[me], peer).start()
@@ -542,6 +558,23 @@
                 HOME, results_out.at[slot_of[away]], results_in.at[me_s], away
             ).start()
     results_in[me_s] = results_out[at_home]
+
+    def sent_et(exchange, source, target):
+        loop(
+            n_et,
+            lambda i: et_copy(exchange, source, target, et_peer(i)).wait_send(),
+        )
+
+    sent_et(FEATURES, res_hbm, features.at[me])
+    sent_et(HEADS, heads_out.at[0], heads_in.at[me])
+    sent_et(MIXED, mixed_out, mixed_in.at[me])
+    for w in range(WAVES):
+        sent_et(PAIRS + w, pairs_out.at[w, 0, 0], pairs_in.at[w, me])
+        sent_et(HIDDEN + w, hidden_out.at[w], hidden_in.at[w, me])
+        for away in others(w):
+            stream_copy(OUTWARD, rows_out.at[0], rows_in.at[0], away).wait_send()
+            stream_copy(HOME, results_out.at[0], results_in.at[0], away).wait_send()
+
     for w in range(WAVES):
         for away in others(w):
             stream_arrival(
@@ -557,22 +590,6 @@
     )
     routed = dot_tn(mixing_high, returned) + dot_tn(mixing_low, returned)
     out_ref[...] = (resid.astype(F32) + routed).astype(BF16)
-
-    def sent_et(exchange, source, target):
-        loop(
-            n_et,
-            lambda i: et_copy(exchange, source, target, et_peer(i)).wait_send(),
-        )
-
-    sent_et(FEATURES, res_hbm, features.at[me])
-    sent_et(HEADS, heads_out.at[0], heads_in.at[me])
-    sent_et(MIXED, mixed_out, mixed_in.at[me])
-    for w in range(WAVES):
-        sent_et(PAIRS + w, pairs_out.at[w, 0, 0], pairs_in.at[w, me])
-        sent_et(HIDDEN + w, hidden_out.at[w], hidden_in.at[w, me])
-        for away in others(w):
-            stream_copy(OUTWARD, rows_out.at[0], rows_in.at[0], away).wait_send()
-            stream_copy(HOME, results_out.at[0], results_in.at[0], away).wait_send()
 
 
 def on_device(
@@ -628,6 +645,8 @@
     pair_width = 2 * hidden + LANES
     share = n_stream // WAVES
     scratch = [vmem(a.shape, a.dtype) for a in args[1:]] + [
+        vmem((span * kv_heads * 2, head_dim), F32),
+        vmem((local, 2, kv_heads // 2, span, 2 * head_dim), BF16),
         vmem((n_et, tokens, features), BF16),
         vmem((n_et, 16, head_dim), BF16),
         vmem((n_et, 16, head_dim), BF16),

time: 57.6 us -> 56.5 us (0.981)
  Pallas kernels: 56.9 us -> 55.9 us
    pallas_call x1, Pallas kernels: 56.9 us -> 55.9 us  [on_device(): pl.pallas_call(functools.partial(kernel, n_stream, n_et), out_shape=pltpu...]
where the time goes in v6:
time: 56.5 us
  Pallas kernels  55.9 us (99%)
  local copies, waits for them, and re-layouts  0.6 us (1%)
    pallas_call x1, Pallas kernels, on_device(): pl.pallas_call(functools.partial(kernel, n_stream, n_et), out_shape=pltpu...  55.9 us

profile of v6, /device:TPU:1, one launch (start us, length us, event | category | flops | bytes accessed | tf_op | source)
XLA Modules:
  0.0 56.5 jit_solution(2399608130239268785)
XLA Ops:
  0.0 55.9 %shard_map.136 = bf16[16,256]{1,0:T(8,128)(2,1)S(1)} custom-call(bf16[16,256]{1,0:T(8,128)(2,1)} %res_hbm.1, bf16[16,128]{1,0:T(8,128)(2,1)} %bitcast.13, bf16[1,128]{1,0:T(2,128)(2,1)} %bitcast.16, bf16[1,128]{1,0:T(2,128)(2,1)} %bitcast.17, bf16[2048,512]{1,0:T(8,128)(2,1)} %w_q_hbm.1, bf16[2048,128]{1,0:T(8,128)(2,1)} %w_kv_hbm.1, ...), custom_call_target="tpu_custom_call" | custom-call | tf_op jit(solution)/shard_map/pallas_call | solution.py:676
  55.9 0.6 %copy.17 = bf16[16,256]{1,0:T(8,128)(2,1)} copy(bf16[16,256]{1,0:T(8,128)(2,1)S(1)} %shard_map.136) | data formatting | bytes 16384

commit v7 on v6

--- a/solution.py
+++ b/solution.py
@@ -248,15 +248,12 @@
 
     load("own", res_hbm, features.at[me])
     load("length", length_hbm, length)
-    load("cache", cache_hbm, cache)
     load("w_q", w_q_hbm, w_q)
     load("w_kv", w_kv_hbm, w_kv)
     load("attn_gain", attn_gain_hbm, attn_gain)
     load("q_gain", q_gain_hbm, q_gain)
     load("key_gain", key_gain_hbm, key_gain)
-    load("ids", ids_hbm, ids)
-    load("gates", gates_hbm, gates)
-    load("moe_gain", moe_gain_hbm, moe_gain)
+    load("cache", cache_hbm, cache)
 
     loads["length"].wait()
     lengths = jnp.broadcast_to(length[...], (tokens, tokens)).astype(F32)
@@ -283,6 +280,56 @@
     )
     order_out = jnp.where(col == picked, 1.0, 0.0).astype(BF16)
 
+    loads["own"].wait()
+    loads["attn_gain"].wait()
+    loop(
+        n_et,
+        lambda i: et_arrival(
+            FEATURES, res_hbm, features.at[et_peer(i)], et_peer(i)
+        ).wait_recv(),
+    )
+    full = jnp.concatenate([features[i].astype(F32) for i in range(n_et)], axis=1)
+    gain = attn_gain[...].astype(F32)
+    gain = jnp.concatenate([gain[i : i + 1] for i in range(gain.shape[0])], axis=1)
+    normed = (
+        full
+        * lax.rsqrt(jnp.sum(full * full, axis=1, keepdims=True) * (1.0 / width) + EPS)
+        * gain
+    ).astype(BF16)
+
+    def rotated(v, g):
+        v = v * lax.rsqrt(jnp.mean(v * v, axis=1, keepdims=True) + EPS) * g
+        return v * cosine + pltpu.roll(v, half, 1) * sine
+
+    loads["q_gain"].wait()
+    loads["key_gain"].wait()
+    loads["w_q"].wait()
+    query = dot(normed, w_q[...])
+    loads["w_kv"].wait()
+    key_value = dot(normed, w_kv[...])
+    query_gain = q_gain[...].astype(F32)
+    made = [
+        rotated(query[:, i * head_dim : (i + 1) * head_dim], query_gain)
+        for i in range(own_heads)
+    ]
+    made.append(
+        jnp.where(me < kv_heads, rotated(key_value, key_gain[...].astype(F32)), key_value)
+    )
+    made.append(jnp.zeros((LANES - (own_heads + 1) * tokens, head_dim), F32))
+    made = jnp.concatenate(made, axis=0).astype(BF16)
+    heads_out[...] = dot(order_out, made).astype(BF16).reshape(heads_out.shape)
+    heads_in[me] = heads_out[me]
+    for peer in et_far_first:
+        et_copy(HEADS, heads_out.at[peer], heads_in.at[me], peer).start()
+    hear(0)
+    tell(1)
+    load("w_o", w_o_hbm, w_o)
+    load("ids", ids_hbm, ids)
+    load("gates", gates_hbm, gates)
+    load("moe_gain", moe_gain_hbm, moe_gain)
+    load("w_gu", w_gu_hbm, w_gu)
+    load("w_down", w_down_hbm, w_down)
+
     per = local * n_heads
     row = iota((3 * per, n_et * pad), 0)
     col = iota((3 * per, n_et * pad), 1)
@@ -294,6 +341,72 @@
         (lax.div(head, group) + jnp.where(kind == 2, kv_heads, 0)) * pad + n_q + token,
     )
     order_in = jnp.where(col == picked, 1.0, 0.0).astype(BF16)
+
+    loads["cache"].wait()
+    rows_of = cache_hbm.shape[0] // local
+    span = rows_of // (2 * kv_heads)
+    for t in range(local):
+        cache_f[...] = cache[t * rows_of : (t + 1) * rows_of, :].astype(F32)
+        for kind in range(2):
+            for h in range(kv_heads):
+                split[t, kind, h // 2, :, h % 2 * head_dim : (h % 2 + 1) * head_dim] = cache_f[
+                    pl.ds(2 * h + kind, span, stride=2 * kv_heads), :
+                ].astype(BF16)
+
+    own_lane = iota((1, tokens), 1)
+    lengths = length[...].astype(F32)
+    pairs = kv_heads // 2
+    column = iota((2 * group, span), 1)
+    live = []
+    for t in range(local):
+        limit = jnp.sum(
+            jnp.where(own_lane == me * local + t, lengths, 0.0), axis=1, keepdims=True
+        ).astype(jnp.int32)
+        live.append(column < limit)
+    empty = jnp.zeros((group, head_dim), F32)
+    loop(
+        n_et,
+        lambda i: et_arrival(
+            HEADS, heads_out.at[et_peer(i)], heads_in.at[et_peer(i)], et_peer(i)
+        ).wait_recv(),
+    )
+    ordered = dot(order_in, heads_in[...].reshape(n_et * pad, head_dim))
+    q = ordered[:per]
+    blocks = []
+    for i in range(local * pairs):
+        at = i * 2 * group
+        upper = jnp.concatenate([q[at : at + group], empty], axis=1)
+        lower = jnp.concatenate([empty, q[at + group : at + 2 * group]], axis=1)
+        blocks.append(jnp.concatenate([upper, lower], axis=0).astype(BF16))
+    scores = [
+        dot_nt(block, split[i // pairs, 0, i % pairs]) for i, block in enumerate(blocks)
+    ]
+    weights = [
+        jnp.where(live[i // pairs], jnp.exp(score * scale), 0.0)
+        for i, score in enumerate(scores)
+    ]
+    summed = [
+        dot(weight.astype(BF16), split[i // pairs, 1, i % pairs])
+        for i, weight in enumerate(weights)
+    ]
+    fresh = jnp.exp(jnp.sum(q * ordered[per : 2 * per], axis=1, keepdims=True) * scale)
+    total = fresh + jnp.concatenate(
+        [jnp.sum(weight, axis=1, keepdims=True) for weight in weights], axis=0
+    )
+    summed = jnp.concatenate(
+        [
+            part
+            for both in summed
+            for part in (both[:group, :head_dim], both[group:, head_dim:])
+        ],
+        axis=0,
+    )
+    mixed_out[...] = ((summed + fresh * ordered[2 * per :]) / total).astype(BF16)
+    mixed_in[me] = mixed_out[...]
+    for peer in et_far_first:
+        et_copy(MIXED, mixed_out, mixed_in.at[me], peer).start()
+    hear(1)
+    tell(2)
 
     loads["ids"].wait()
     loads["gates"].wait()
@@ -318,119 +431,6 @@
     placed = placed.astype(BF16)
     mixing_high = mixing.astype(BF16)
     mixing_low = (mixing - mixing_high.astype(F32)).astype(BF16)
-
-    loads["cache"].wait()
-    rows_of = cache_hbm.shape[0] // local
-    span = rows_of // (2 * kv_heads)
-    for t in range(local):
-        cache_f[...] = cache[t * rows_of : (t + 1) * rows_of, :].astype(F32)
-        for kind in range(2):
-            for h in range(kv_heads):
-                split[t, kind, h // 2, :, h % 2 * head_dim : (h % 2 + 1) * head_dim] = cache_f[
-                    pl.ds(2 * h + kind, span, stride=2 * kv_heads), :
-                ].astype(BF16)
-
-    loads["own"].wait()
-    loads["attn_gain"].wait()
-    loop(
-        n_et,
-        lambda i: et_arrival(
-            FEATURES, res_hbm, features.at[et_peer(i)], et_peer(i)
-        ).wait_recv(),
-    )
-    full = jnp.concatenate([features[i].astype(F32) for i in range(n_et)], axis=1)
-    gain = attn_gain[...].astype(F32)
-    gain = jnp.concatenate([gain[i : i + 1] for i in range(gain.shape[0])], axis=1)
-    normed = (
-        full
-        * lax.rsqrt(jnp.sum(full * full, axis=1, keepdims=True) * (1.0 / width) + EPS)
-        * gain
-    ).astype(BF16)
-
-    def rotated(v, g):
-        v = v * lax.rsqrt(jnp.mean(v * v, axis=1, keepdims=True) + EPS) * g
-        return v * cosine + pltpu.roll(v, half, 1) * sine
-
-    loads["q_gain"].wait()
-    loads["key_gain"].wait()
-    loads["w_q"].wait()
-    query = dot(normed, w_q[...])
-    loads["w_kv"].wait()
-    key_value = dot(normed, w_kv[...])
-    query_gain = q_gain[...].astype(F32)
-    made = [
-        rotated(query[:, i * head_dim : (i + 1) * head_dim], query_gain)
-        for i in range(own_heads)
-    ]
-    made.append(
-        jnp.where(me < kv_heads, rotated(key_value, key_gain[...].astype(F32)), key_value)
-    )
-    made.append(jnp.zeros((LANES - (own_heads + 1) * tokens, head_dim), F32))
-    made = jnp.concatenate(made, axis=0).astype(BF16)
-    heads_out[...] = dot(order_out, made).astype(BF16).reshape(heads_out.shape)
-    heads_in[me] = heads_out[me]
-    for peer in et_far_first:
-        et_copy(HEADS, heads_out.at[peer], heads_in.at[me], peer).start()
-    hear(0)
-    tell(1)
-    load("w_o", w_o_hbm, w_o)
-    load("w_gu", w_gu_hbm, w_gu)
-    load("w_down", w_down_hbm, w_down)
-
-    own_lane = iota((1, tokens), 1)
-    lengths = length[...].astype(F32)
-    pairs = kv_heads // 2
-    column = iota((2 * group, span), 1)
-    live = []
-    for t in range(local):
-        limit = jnp.sum(
-            jnp.where(own_lane == me * local + t, lengths, 0.0), axis=1, keepdims=True
-        ).astype(jnp.int32)
-        live.append(column < limit)
-    empty = jnp.zeros((group, head_dim), F32)
-    loop(
-        n_et,
-        lambda i: et_arrival(
-            HEADS, heads_out.at[et_peer(i)], heads_in.at[et_peer(i)], et_peer(i)
-        ).wait_recv(),
-    )
-    ordered = dot(order_in, heads_in[...].reshape(n_et * pad, head_dim))
-    q = ordered[:per]
-    blocks = []
-    for i in range(local * pairs):
-        at = i * 2 * group
-        upper = jnp.concatenate([q[at : at + group], empty], axis=1)
-        lower = jnp.concatenate([empty, q[at + group : at + 2 * group]], axis=1)
-        blocks.append(jnp.concatenate([upper, lower], axis=0).astype(BF16))
-    scores = [
-        dot_nt(block, split[i // pairs, 0, i % pairs]) for i, block in enumerate(blocks)
-    ]
-    weights = [
-        jnp.where(live[i // pairs], jnp.exp(score * scale), 0.0)
-        for i, score in enumerate(scores)
-    ]
-    summed = [
-        dot(weight.astype(BF16), split[i // pairs, 1, i % pairs])
-        for i, weight in enumerate(weights)
-    ]
-    fresh = jnp.exp(jnp.sum(q * ordered[per : 2 * per], axis=1, keepdims=True) * scale)
-    total = fresh + jnp.concatenate(
-        [jnp.sum(weight, axis=1, keepdims=True) for weight in weights], axis=0
-    )
-    summed = jnp.concatenate(
-        [
-            part
-            for both in summed
-            for part in (both[:group, :head_dim], both[group:, head_dim:])
-        ],
-        axis=0,
-    )
-    mixed_out[...] = ((summed + fresh * ordered[2 * per :]) / total).astype(BF16)
-    mixed_in[me] = mixed_out[...]
-    for peer in et_far_first:
-        et_copy(MIXED, mixed_out, mixed_in.at[me], peer).start()
-    hear(1)
-    tell(2)
 
     loads["w_o"].wait()
     loop(
@@ -503,7 +503,7 @@
             )
             pairs_out[w, i] = products.astype(BF16).reshape(pairs_out.shape[2:])
             if i < n_local - 1:
-                for c in range(CAP):
+                for c in (y_low, 1 - y_low):
                     et_copy(
                         PAIRS + w, pairs_out.at[w, i, c], pairs_in.at[w, me], CAP * j + c
                     ).start()

time: 56.5 us -> 55.9 us (0.989)
  Pallas kernels: 55.9 us -> 55.1 us
    pallas_call x1, Pallas kernels: 55.9 us -> 55.1 us  [on_device(): pl.pallas_call(functools.partial(kernel, n_stream, n_et), out_shape=pltpu...]
where the time goes in v7:
time: 55.9 us; the launch traced here: 55.7 us
  Pallas kernels  55.1 us (99%)
  local copies, waits for them, and re-layouts  0.6 us (1%)
    pallas_call x1, Pallas kernels, on_device(): pl.pallas_call(functools.partial(kernel, n_stream, n_et), out_shape=pltpu...  55.1 us

profile of v7, /device:TPU:1, one launch (start us, length us, event | category | flops | bytes accessed | tf_op | source)
XLA Modules:
  0.0 55.7 jit_solution(4510652198539788074)
XLA Ops:
  0.0 55.1 %shard_map.136 = bf16[16,256]{1,0:T(8,128)(2,1)S(1)} custom-call(bf16[16,256]{1,0:T(8,128)(2,1)} %res_hbm.1, bf16[16,128]{1,0:T(8,128)(2,1)} %bitcast.13, bf16[1,128]{1,0:T(2,128)(2,1)} %bitcast.16, bf16[1,128]{1,0:T(2,128)(2,1)} %bitcast.17, bf16[2048,512]{1,0:T(8,128)(2,1)} %w_q_hbm.1, bf16[2048,128]{1,0:T(8,128)(2,1)} %w_kv_hbm.1, ...), custom_call_target="tpu_custom_call" | custom-call | tf_op jit(solution)/shard_map/pallas_call | solution.py:676
  55.1 0.6 %copy.17 = bf16[16,256]{1,0:T(8,128)(2,1)} copy(bf16[16,256]{1,0:T(8,128)(2,1)S(1)} %shard_map.136) | data formatting | bytes 16384

commit v8 on v7

--- a/solution.py
+++ b/solution.py
@@ -154,20 +154,38 @@
     def hops(away):
         return min(away[1], n_z - away[1]) + 2 * away[0]
 
-    def back(away):
-        return (-away[0] % n_y, -away[1] % n_z, -away[2] % n_core)
-
-    relative = sorted(
-        [(dy, dz, dc) for dy in range(n_y) for dz in range(n_z) for dc in range(n_core)],
-        key=lambda away: (hops(away), away != (0, 0, 0)),
-    )
+    others = sorted(
+        [
+            (dy, dz, dc)
+            for dy in range(n_y)
+            for dz in range(n_z)
+            for dc in range(n_core)
+            if dy or dz or dc
+        ],
+        key=lambda away: -hops(away),
+    )
+
     share = n_stream // WAVES
-    waves = [
-        sorted(relative[w * share : (w + 1) * share], key=lambda away: -hops(away))
-        for w in range(WAVES)
-    ]
-    slot_of = {away: i for i, away in enumerate(waves[0] + waves[1])}
-    at_home = slot_of[0, 0, 0]
+    deep = n_z // WAVES
+
+    def slot_of(stream):
+        y, z, core = stream // (n_z * n_core), stream // n_core % n_z, stream % n_core
+        return z // deep * share + (y * deep + z % deep) * n_core + core
+
+    stream_in = {slot_of(i): i for i in range(n_stream)}
+    at_home = slot_of(me_s)
+
+    def members(w):
+        return [
+            (
+                lax.rem(y + dy, n_y) * (n_z * n_core)
+                + (w * deep + lax.rem(z + dz, deep)) * n_core
+                + lax.rem(core + dc, n_core)
+            )
+            for dy in reversed(range(n_y))
+            for dz in reversed(range(deep))
+            for dc in reversed(range(n_core))
+        ]
 
     n_x = n_et // 2
     x, y_low = lax.div(me, 2), lax.rem(me, 2)
@@ -198,28 +216,21 @@
             device_id_type=MESH,
         )
 
-    def stream_copy(exchange, source, target, away):
+    def stream_copy(exchange, source, target, peer):
         return pltpu.make_async_remote_copy(
             src_ref=source,
             dst_ref=target,
-            send_sem=stream_send.at[exchange, slot_of[away]],
-            recv_sem=stream_recv.at[exchange, slot_of[back(away)]],
-            device_id=(stream_at(*away), me),
+            send_sem=stream_send.at[exchange, slot_of(peer)],
+            recv_sem=stream_recv.at[exchange, at_home],
+            device_id=(peer, me),
             device_id_type=MESH,
         )
 
-    def stream_arrival(exchange, source, target, away):
-        return pltpu.make_async_remote_copy(
-            src_ref=source,
-            dst_ref=target,
-            send_sem=stream_send.at[exchange, slot_of[away]],
-            recv_sem=stream_recv.at[exchange, slot_of[away]],
-            device_id=(stream_at(*away), me),
-            device_id_type=MESH,
-        )
-
-    def others(wave):
-        return [away for away in waves[wave] if away != (0, 0, 0)]
+    def stream_arrival(exchange, source, target, slot):
+        return pltpu.make_async_copy(source, target, stream_recv.at[exchange, slot])
+
+    def unless_home(w, body):
+        pl.when(lax.div(z, deep) != w)(body)
 
     def loop(n, body):
         def step(i, carry):
@@ -450,16 +461,11 @@
     rows_out[...] = jnp.concatenate(
         [sent[:, :, :LANES], sent[:, :, LANES:]], axis=1
     ).astype(BF16)
-    rows_in[at_home] = rows_out[me_s]
     hear(2)
-    for w in range(WAVES):
-        for away in others(w):
-            stream_copy(
-                OUTWARD,
-                rows_out.at[stream_at(*away)],
-                rows_in.at[slot_of[back(away)]],
-                away,
-            ).start()
+    for away in others:
+        peer = stream_at(*away)
+        stream_copy(OUTWARD, rows_out.at[peer], rows_in.at[at_home], peer).start()
+    stream_arrival(OUTWARD, rows_out.at[me_s], rows_in.at[at_home], at_home).start()
     loads["moe_gain"].wait()
     gain = moe_gain[...].astype(F32)
     gain = jnp.concatenate([gain[0:1], gain[1:2]], axis=1)
@@ -468,10 +474,8 @@
     hidden_width = w_down_hbm.shape[1]
 
     for w in range(WAVES):
-        for away in others(w):
-            stream_arrival(
-                OUTWARD, rows_out.at[0], rows_in.at[slot_of[away]], away
-            ).wait_recv()
+        for slot in range(w * share, (w + 1) * share):
+            stream_arrival(OUTWARD, rows_out.at[0], rows_in.at[slot], slot).wait()
         rows_f[w * share * chunk : (w + 1) * share * chunk, :] = (
             rows_in[w * share : (w + 1) * share].reshape(share * chunk, LANES).astype(F32)
         )
@@ -553,11 +557,18 @@
             .astype(BF16)
             .reshape(share, chunk, LANES)
         )
-        for away in others(w):
+        *rest, last = members(w)
+        for peer in rest:
             stream_copy(
-                HOME, results_out.at[slot_of[away]], results_in.at[me_s], away
+                HOME, results_out.at[slot_of(peer)], results_in.at[me_s], peer
             ).start()
-    results_in[me_s] = results_out[at_home]
+        unless_home(
+            w,
+            lambda: stream_copy(
+                HOME, results_out.at[slot_of(last)], results_in.at[me_s], last
+            ).start(),
+        )
+    stream_arrival(HOME, results_out.at[at_home], results_in.at[me_s], at_home).start()
 
     def sent_et(exchange, source, target):
         loop(
@@ -571,15 +582,25 @@
     for w in range(WAVES):
         sent_et(PAIRS + w, pairs_out.at[w, 0, 0], pairs_in.at[w, me])
         sent_et(HIDDEN + w, hidden_out.at[w], hidden_in.at[w, me])
-        for away in others(w):
-            stream_copy(OUTWARD, rows_out.at[0], rows_in.at[0], away).wait_send()
-            stream_copy(HOME, results_out.at[0], results_in.at[0], away).wait_send()
-
+    for away in others:
+        stream_copy(
+            OUTWARD, rows_out.at[0], rows_in.at[at_home], stream_at(*away)
+        ).wait_send()
     for w in range(WAVES):
-        for away in others(w):
-            stream_arrival(
-                HOME, results_out.at[0], results_in.at[stream_at(*away)], away
-            ).wait_recv()
+        *rest, last = members(w)
+        for peer in rest:
+            stream_copy(HOME, results_out.at[0], results_in.at[me_s], peer).wait_send()
+        unless_home(
+            w,
+            lambda: stream_copy(
+                HOME, results_out.at[0], results_in.at[me_s], last
+            ).wait_send(),
+        )
+
+    for slot in range(n_stream):
+        stream_arrival(
+            HOME, results_out.at[0], results_in.at[stream_in[slot]], slot
+        ).wait()
     returned = results_in[...].astype(F32)
     returned = (
         jnp.concatenate(

time: 55.9 us -> 53.6 us (0.959)
  Pallas kernels: 55.1 us -> 52.8 us
    pallas_call x1, Pallas kernels: 55.1 us -> 52.8 us  [on_device(): pl.pallas_call(functools.partial(kernel, n_stream, n_et), out_shape=pltpu...]
where the time goes in v8:
time: 53.6 us; the launch traced here: 53.4 us
  Pallas kernels  52.8 us (99%)
  local copies, waits for them, and re-layouts  0.6 us (1%)
    pallas_call x1, Pallas kernels, on_device(): pl.pallas_call(functools.partial(kernel, n_stream, n_et), out_shape=pltpu...  52.8 us

profile of v8, /device:TPU:1, one launch (start us, length us, event | category | flops | bytes accessed | tf_op | source)
XLA Modules:
  0.0 53.4 jit_solution(1855913396031143872)
XLA Ops:
  0.0 52.8 %shard_map.136 = bf16[16,256]{1,0:T(8,128)(2,1)S(1)} custom-call(bf16[16,256]{1,0:T(8,128)(2,1)} %res_hbm.1, bf16[16,128]{1,0:T(8,128)(2,1)} %bitcast.13, bf16[1,128]{1,0:T(2,128)(2,1)} %bitcast.16, bf16[1,128]{1,0:T(2,128)(2,1)} %bitcast.17, bf16[2048,512]{1,0:T(8,128)(2,1)} %w_q_hbm.1, bf16[2048,128]{1,0:T(8,128)(2,1)} %w_kv_hbm.1, ...), custom_call_target="tpu_custom_call" | custom-call | tf_op jit(solution)/shard_map/pallas_call | solution.py:697
  52.8 0.6 %copy.17 = bf16[16,256]{1,0:T(8,128)(2,1)} copy(bf16[16,256]{1,0:T(8,128)(2,1)S(1)} %shard_map.136) | data formatting | bytes 16384

commit v9 on v8

--- a/solution.py
+++ b/solution.py
@@ -16,9 +16,12 @@
 F32 = jnp.float32
 BF16 = jnp.bfloat16
 
-FEATURES, HEADS, MIXED, PAIRS, HIDDEN = 0, 1, 2, 3, 5
+FEATURES, HEADS, MIXED, PAIRS, HIDDEN = 0, 1, 2, 3, 7
 OUTWARD, HOME = range(2)
-WAVES = 2
+
+
+def parts_of(n_stream):
+    return 4 if n_stream % 16 == 0 else 2
 
 
 def iota(shape, dim):
@@ -81,9 +84,11 @@
     rows_f,
     expert_rows,
     expert_squares,
-    pairs_out,
+    pairs_even,
+    pairs_odd,
     pairs_own,
-    pairs_in,
+    pairs_in_even,
+    pairs_in_odd,
     hidden_out,
     hidden_in,
     results_f,
@@ -151,41 +156,36 @@
         if number < len(rounds):
             pl.semaphore_wait(known.at[number], len(rounds[number]))
 
-    def hops(away):
-        return min(away[1], n_z - away[1]) + 2 * away[0]
-
-    others = sorted(
-        [
-            (dy, dz, dc)
-            for dy in range(n_y)
-            for dz in range(n_z)
-            for dc in range(n_core)
-            if dy or dz or dc
-        ],
-        key=lambda away: -hops(away),
-    )
-
-    share = n_stream // WAVES
-    deep = n_z // WAVES
+    parts = parts_of(n_stream)
+    n_waves = parts // 2
+    share, small = n_stream // n_waves, n_stream // parts
+    deep = n_z // parts
+    own_part = lax.div(z, deep)
 
     def slot_of(stream):
         y, z, core = stream // (n_z * n_core), stream // n_core % n_z, stream % n_core
-        return z // deep * share + (y * deep + z % deep) * n_core + core
+        return z // deep * small + (y * deep + z % deep) * n_core + core
 
     stream_in = {slot_of(i): i for i in range(n_stream)}
-    at_home = slot_of(me_s)
-
-    def members(w):
-        return [
-            (
-                lax.rem(y + dy, n_y) * (n_z * n_core)
-                + (w * deep + lax.rem(z + dz, deep)) * n_core
-                + lax.rem(core + dc, n_core)
-            )
-            for dy in reversed(range(n_y))
-            for dz in reversed(range(deep))
-            for dc in reversed(range(n_core))
-        ]
+    at_home = own_part * small + (y * deep + lax.rem(z, deep)) * n_core + core
+
+    def members(part):
+        found = []
+        for dy in reversed(range(n_y)):
+            for dz in reversed(range(deep)):
+                for dc in reversed(range(n_core)):
+                    at_y, at_z, at_core = (
+                        lax.rem(y + dy, n_y),
+                        lax.rem(z + dz, deep),
+                        lax.rem(core + dc, n_core),
+                    )
+                    found.append(
+                        (
+                            at_y * (n_z * n_core) + (part * deep + at_z) * n_core + at_core,
+                            part * small + (at_y * deep + at_z) * n_core + at_core,
+                        )
+                    )
+        return found
 
     n_x = n_et // 2
     x, y_low = lax.div(me, 2), lax.rem(me, 2)
@@ -216,11 +216,11 @@
             device_id_type=MESH,
         )
 
-    def stream_copy(exchange, source, target, peer):
+    def stream_copy(exchange, number, source, target, peer):
         return pltpu.make_async_remote_copy(
             src_ref=source,
             dst_ref=target,
-            send_sem=stream_send.at[exchange, slot_of(peer)],
+            send_sem=stream_send.at[exchange, number],
             recv_sem=stream_recv.at[exchange, at_home],
             device_id=(peer, me),
             device_id_type=MESH,
@@ -229,8 +229,8 @@
     def stream_arrival(exchange, source, target, slot):
         return pltpu.make_async_copy(source, target, stream_recv.at[exchange, slot])
 
-    def unless_home(w, body):
-        pl.when(lax.div(z, deep) != w)(body)
+    def unless_home(part, body):
+        pl.when(own_part != part)(body)
 
     def loop(n, body):
         def step(i, carry):
@@ -238,6 +238,14 @@
             return carry
 
         lax.fori_loop(1, n, step, 0)
+
+    loads = {}
+
+    def load(name, source, target):
+        loads[name] = pltpu.make_async_copy(source, target, load_sem.at[len(loads)])
+        loads[name].start()
+
+    load("own", res_hbm, features.at[me])
 
     barrier = pltpu.get_barrier_semaphore()
     greeted = [(me_s, peer) for peer in et_far_first]
@@ -247,17 +255,11 @@
 
     pl.semaphore_wait(barrier, len(greeted))
 
+    loads["own"].wait()
     for peer in et_far_first:
-        et_copy(FEATURES, res_hbm, features.at[me], peer).start()
+        et_copy(FEATURES, features.at[me], features.at[me], peer).start()
     tell(0)
 
-    loads = {}
-
-    def load(name, source, target):
-        loads[name] = pltpu.make_async_copy(source, target, load_sem.at[len(loads)])
-        loads[name].start()
-
-    load("own", res_hbm, features.at[me])
     load("length", length_hbm, length)
     load("w_q", w_q_hbm, w_q)
     load("w_kv", w_kv_hbm, w_kv)
@@ -270,12 +272,12 @@
     lengths = jnp.broadcast_to(length[...], (tokens, tokens)).astype(F32)
     diagonal = iota((tokens, tokens), 0) == iota((tokens, tokens), 1)
     positions = jnp.sum(jnp.where(diagonal, lengths, 0.0), axis=1, keepdims=True)
-    half = head_dim // 2
+    turn = head_dim // 2
     lane = iota((tokens, head_dim), 1)
-    steps = jnp.where(lane < half, lane, lane - half).astype(F32)
+    steps = jnp.where(lane < turn, lane, lane - turn).astype(F32)
     angle = positions * jnp.exp(steps * (-2.0 * math.log(ROPE_BASE) / head_dim))
     cosine = jnp.cos(angle)
-    sine = jnp.where(lane < half, -jnp.sin(angle), jnp.sin(angle))
+    sine = jnp.where(lane < turn, -jnp.sin(angle), jnp.sin(angle))
 
     pad = 16
     row = iota((n_et * pad, LANES), 0)
@@ -291,7 +293,6 @@
     )
     order_out = jnp.where(col == picked, 1.0, 0.0).astype(BF16)
 
-    loads["own"].wait()
     loads["attn_gain"].wait()
     loop(
         n_et,
@@ -310,7 +311,7 @@
 
     def rotated(v, g):
         v = v * lax.rsqrt(jnp.mean(v * v, axis=1, keepdims=True) + EPS) * g
-        return v * cosine + pltpu.roll(v, half, 1) * sine
+        return v * cosine + pltpu.roll(v, turn, 1) * sine
 
     loads["q_gain"].wait()
     loads["key_gain"].wait()
@@ -462,9 +463,13 @@
         [sent[:, :, :LANES], sent[:, :, LANES:]], axis=1
     ).astype(BF16)
     hear(2)
-    for away in others:
-        peer = stream_at(*away)
-        stream_copy(OUTWARD, rows_out.at[peer], rows_in.at[at_home], peer).start()
+    beside = own_part + 1 - 2 * lax.rem(own_part, 2)
+    order = [beside, own_part]
+    if parts == 4:
+        order = [lax.rem(part + 2, parts) for part in order] + order
+    outward = [peer for part in order for peer, _ in members(part)][:-1]
+    for number, peer in enumerate(outward):
+        stream_copy(OUTWARD, number, rows_out.at[peer], rows_in.at[at_home], peer).start()
     stream_arrival(OUTWARD, rows_out.at[me_s], rows_in.at[at_home], at_home).start()
     loads["moe_gain"].wait()
     gain = moe_gain[...].astype(F32)
@@ -473,70 +478,88 @@
     chunk = 2 * n_local * CAP
     hidden_width = w_down_hbm.shape[1]
 
-    for w in range(WAVES):
-        for slot in range(w * share, (w + 1) * share):
+    left_lanes = iota((CAP * small, LANES), 1) < LANES // 2
+    for part in range(parts):
+        w, odd = part // 2, part % 2
+        for slot in range(part * small, (part + 1) * small):
             stream_arrival(OUTWARD, rows_out.at[0], rows_in.at[slot], slot).wait()
-        rows_f[w * share * chunk : (w + 1) * share * chunk, :] = (
-            rows_in[w * share : (w + 1) * share].reshape(share * chunk, LANES).astype(F32)
+        rows_f[part * small * chunk : (part + 1) * small * chunk, :] = (
+            rows_in[part * small : (part + 1) * small].reshape(small * chunk, LANES).astype(F32)
         )
         for j in range(n_local):
             taken = []
             for c in range(CAP):
-                first = w * share * chunk + c * n_local + j
+                first = part * small * chunk + c * n_local + j
                 taken.append(
                     jnp.concatenate(
                         [
-                            rows_f[pl.ds(first + h * n_local * CAP, share, stride=chunk), :]
+                            rows_f[pl.ds(first + h * n_local * CAP, small, stride=chunk), :]
                             for h in range(2)
                         ],
                         axis=1,
                     )
                 )
             taken = jnp.concatenate(taken, axis=0)
-            squares = jnp.sum(taken * taken, axis=1, keepdims=True)
-            high = squares.astype(BF16).astype(F32)
-            expert_squares[w, j] = jnp.where(
-                iota((CAP * share, LANES), 1) < LANES // 2, high, squares - high
+            expert_squares[part, j] = jnp.broadcast_to(
+                jnp.sum(taken * taken, axis=1, keepdims=True), (CAP * small, LANES)
             )
-            expert_rows[w, j] = (taken * gain).astype(BF16)
+            expert_rows[part, j] = (taken * gain).astype(BF16)
+        sent, received = (pairs_odd, pairs_in_odd) if odd else (pairs_even, pairs_in_even)
         for i in range(n_local):
             j = lax.rem(lax.div(me, CAP) + (2, 1, 3, 0)[i], n_local)
-            taken = expert_rows[w, j]
-            products = jnp.concatenate(
-                [dot(taken, w_gu[j, 0]), dot(taken, w_gu[j, 1]), expert_squares[w, j]], axis=1
+            taken = expert_rows[part, j]
+            halves = [dot(taken, w_gu[j, 0]), dot(taken, w_gu[j, 1])]
+            if odd:
+                squares = jnp.where(
+                    left_lanes, expert_squares[part - 1, j], expert_squares[part, j]
+                )
+                high = squares.astype(BF16).astype(F32)
+                halves = [
+                    jnp.concatenate([halves[0], high], axis=1),
+                    jnp.concatenate([halves[1], squares - high], axis=1),
+                ]
+            for c in range(CAP):
+                products = jnp.concatenate(
+                    [value[c * small : (c + 1) * small] for value in halves], axis=0
+                )
+                sent[w, i, c] = products.astype(BF16)
+                if i == n_local - 1:
+                    pairs_own[part, c, :, : products.shape[1]] = products
+            for c in (y_low, 1 - y_low) if i < n_local - 1 else (1 - y_low,):
+                et_copy(
+                    PAIRS + part, sent.at[w, i, c], received.at[w, me], CAP * j + c
+                ).start()
+    for w in range(n_waves):
+        sums = []
+        for part in (2 * w, 2 * w + 1):
+            odd = part % 2
+            sent, received = (pairs_odd, pairs_in_odd) if odd else (pairs_even, pairs_in_even)
+            pair = pairs_own[part, y_low, :, : received.shape[3]]
+            for i in range(1, n_et):
+                et_arrival(
+                    PAIRS + part, sent.at[w, 0, 0], received.at[w, et_peer(i)], et_peer(i)
+                ).wait_recv()
+                pair = pair + received[w, et_peer(i)].astype(F32)
+            sums.append(pair)
+        squares = sums[1][:small, hidden_width:] + sums[1][small:, hidden_width:]
+        left = iota((small, LANES), 1) < LANES // 2
+        made = []
+        for pair, lanes in zip(sums, (left, ~left)):
+            level = lax.rsqrt(
+                jnp.sum(jnp.where(lanes, squares, 0.0), axis=1, keepdims=True)
+                * (2.0 / LANES / width)
+                + EPS
             )
-            pairs_out[w, i] = products.astype(BF16).reshape(pairs_out.shape[2:])
-            if i < n_local - 1:
-                for c in (y_low, 1 - y_low):
-                    et_copy(
-                        PAIRS + w, pairs_out.at[w, i, c], pairs_in.at[w, me], CAP * j + c
-                    ).start()
-            else:
-                pairs_own[w] = products.reshape(pairs_own.shape[1:])
-                c = 1 - lax.rem(me, CAP)
-                et_copy(
-                    PAIRS + w, pairs_out.at[w, i, c], pairs_in.at[w, me], CAP * j + c
-                ).start()
-    for w in range(WAVES):
-        pair = pairs_own[w, lax.rem(me, CAP)]
-        for i in range(1, n_et):
-            et_arrival(
-                PAIRS + w, pairs_out.at[w, 0, 0], pairs_in.at[w, et_peer(i)], et_peer(i)
-            ).wait_recv()
-            pair = pair + pairs_in[w, et_peer(i)].astype(F32)
-        squares = jnp.sum(pair[:, 2 * hidden_width :], axis=1, keepdims=True) * (
-            2.0 / LANES / width
-        )
-        level = lax.rsqrt(squares + EPS)
-        first = pair[:, :hidden_width] * level
-        second = pair[:, hidden_width : 2 * hidden_width] * level
-        hidden_out[w] = (first / (1.0 + jnp.exp(-first)) * second).astype(BF16)
+            first = pair[:small, :hidden_width] * level
+            second = pair[small:, :hidden_width] * level
+            made.append(first / (1.0 + jnp.exp(-first)) * second)
+        hidden_out[w] = jnp.concatenate(made, axis=0).astype(BF16)
         for peer in et_far_first:
             et_copy(HIDDEN + w, hidden_out.at[w], hidden_in.at[w, me], peer).start()
         hidden_in[w, me] = hidden_out[w]
 
     loads["w_down"].wait()
-    for w in range(WAVES):
+    for w in range(n_waves):
         loop(
             n_et,
             lambda i: et_arrival(
@@ -557,17 +580,18 @@
             .astype(BF16)
             .reshape(share, chunk, LANES)
         )
-        *rest, last = members(w)
-        for peer in rest:
-            stream_copy(
-                HOME, results_out.at[slot_of(peer)], results_in.at[me_s], peer
-            ).start()
-        unless_home(
-            w,
-            lambda: stream_copy(
-                HOME, results_out.at[slot_of(last)], results_in.at[me_s], last
-            ).start(),
-        )
+        for part in (2 * w, 2 * w + 1):
+            *rest, (last, place) = members(part)
+            for number, (peer, slot) in enumerate(rest):
+                stream_copy(
+                    HOME, part * small + number, results_out.at[slot], results_in.at[me_s], peer
+                ).start()
+            unless_home(
+                part,
+                lambda: stream_copy(
+                    HOME, (part + 1) * small - 1, results_out.at[place], results_in.at[me_s], last
+                ).start(),
+            )
     stream_arrival(HOME, results_out.at[at_home], results_in.at[me_s], at_home).start()
 
     def sent_et(exchange, source, target):
@@ -576,24 +600,26 @@
             lambda i: et_copy(exchange, source, target, et_peer(i)).wait_send(),
         )
 
-    sent_et(FEATURES, res_hbm, features.at[me])
+    sent_et(FEATURES, features.at[me], features.at[me])
     sent_et(HEADS, heads_out.at[0], heads_in.at[me])
     sent_et(MIXED, mixed_out, mixed_in.at[me])
-    for w in range(WAVES):
-        sent_et(PAIRS + w, pairs_out.at[w, 0, 0], pairs_in.at[w, me])
+    for part in range(parts):
+        sent, received = (pairs_odd, pairs_in_odd) if part % 2 else (pairs_even, pairs_in_even)
+        sent_et(PAIRS + part, sent.at[part // 2, 0, 0], received.at[part // 2, me])
+    for w in range(n_waves):
         sent_et(HIDDEN + w, hidden_out.at[w], hidden_in.at[w, me])
-    for away in others:
-        stream_copy(
-            OUTWARD, rows_out.at[0], rows_in.at[at_home], stream_at(*away)
-        ).wait_send()
-    for w in range(WAVES):
-        *rest, last = members(w)
-        for peer in rest:
-            stream_copy(HOME, results_out.at[0], results_in.at[me_s], peer).wait_send()
+    for number, peer in enumerate(outward):
+        stream_copy(OUTWARD, number, rows_out.at[0], rows_in.at[at_home], peer).wait_send()
+    for part in range(parts):
+        *rest, (last, _) = members(part)
+        for number, (peer, _) in enumerate(rest):
+            stream_copy(
+                HOME, part * small + number, results_out.at[0], results_in.at[me_s], peer
+            ).wait_send()
         unless_home(
-            w,
+            part,
             lambda: stream_copy(
-                HOME, results_out.at[0], results_in.at[me_s], last
+                HOME, (part + 1) * small - 1, results_out.at[0], results_in.at[me_s], last
             ).wait_send(),
         )
 
@@ -663,8 +689,9 @@
     vmem = pltpu.VMEM
     row_blocks = (n_stream, chunk, LANES)
     flat_rows = (n_stream * chunk, LANES)
-    pair_width = 2 * hidden + LANES
-    share = n_stream // WAVES
+    parts = parts_of(n_stream)
+    n_waves = parts // 2
+    share, small = n_stream // n_waves, n_stream // parts
     scratch = [vmem(a.shape, a.dtype) for a in args[1:]] + [
         vmem((span * kv_heads * 2, head_dim), F32),
         vmem((local, 2, kv_heads // 2, span, 2 * head_dim), BF16),
@@ -677,19 +704,21 @@
         vmem(row_blocks, BF16),
         vmem(row_blocks, BF16),
         vmem(flat_rows, F32),
-        vmem((WAVES, n_local, CAP * share, features), BF16),
-        vmem((WAVES, n_local, CAP * share, LANES), F32),
-        vmem((WAVES, n_local, CAP, share, pair_width), BF16),
-        vmem((WAVES, CAP, share, pair_width), F32),
-        vmem((WAVES, n_et, share, pair_width), BF16),
-        vmem((WAVES, share, hidden), BF16),
-        vmem((WAVES, n_et, share, hidden), BF16),
+        vmem((parts, n_local, CAP * small, features), BF16),
+        vmem((parts, n_local, CAP * small, LANES), F32),
+        vmem((n_waves, n_local, CAP, 2 * small, hidden), BF16),
+        vmem((n_waves, n_local, CAP, 2 * small, hidden + LANES), BF16),
+        vmem((parts, CAP, 2 * small, hidden + LANES), F32),
+        vmem((n_waves, n_et, 2 * small, hidden), BF16),
+        vmem((n_waves, n_et, 2 * small, hidden + LANES), BF16),
+        vmem((n_waves, share, hidden), BF16),
+        vmem((n_waves, n_et, share, hidden), BF16),
         vmem(flat_rows, F32),
         vmem(row_blocks, BF16),
         vmem(row_blocks, BF16),
         pltpu.SemaphoreType.DMA((len(args),)),
-        pltpu.SemaphoreType.DMA((7, n_et)),
-        pltpu.SemaphoreType.DMA((7, n_et)),
+        pltpu.SemaphoreType.DMA((9, n_et)),
+        pltpu.SemaphoreType.DMA((9, n_et)),
         pltpu.SemaphoreType.DMA((2, n_stream)),
         pltpu.SemaphoreType.DMA((2, n_stream)),
         pltpu.SemaphoreType.REGULAR((3,)),

time: 53.6 us -> 53.1 us (level)
  no operation moved by 1% of the time
where the time goes in v9:
time: 53.1 us; the launch traced here: 53 us
  Pallas kernels  52.4 us (99%)
  local copies, waits for them, and re-layouts  0.6 us (1%)
    pallas_call x1, Pallas kernels, on_device(): pl.pallas_call(functools.partial(kernel, n_stream, n_et), out_shape=pltpu...  52.4 us

profile of v9, /device:TPU:1, one launch (start us, length us, event | category | flops | bytes accessed | tf_op | source)
XLA Modules:
  0.0 53.0 jit_solution(13287710507852550051)
XLA Ops:
  0.0 52.4 %shard_map.136 = bf16[16,256]{1,0:T(8,128)(2,1)S(1)} custom-call(bf16[16,256]{1,0:T(8,128)(2,1)} %res_hbm.1, bf16[16,128]{1,0:T(8,128)(2,1)} %bitcast.13, bf16[1,128]{1,0:T(2,128)(2,1)} %bitcast.16, bf16[1,128]{1,0:T(2,128)(2,1)} %bitcast.17, bf16[2048,512]{1,0:T(8,128)(2,1)} %w_q_hbm.1, bf16[2048,128]{1,0:T(8,128)(2,1)} %w_kv_hbm.1, ...), custom_call_target="tpu_custom_call" | custom-call | tf_op jit(solution)/shard_map/pallas_call | solution.py:726
  52.4 0.6 %copy.17 = bf16[16,256]{1,0:T(8,128)(2,1)} copy(bf16[16,256]{1,0:T(8,128)(2,1)S(1)} %shard_map.136) | data formatting | bytes 16384

commit v10 on v9

--- a/solution.py
+++ b/solution.py
@@ -358,7 +358,7 @@
     rows_of = cache_hbm.shape[0] // local
     span = rows_of // (2 * kv_heads)
     for t in range(local):
-        cache_f[...] = cache[t * rows_of : (t + 1) * rows_of, :].astype(F32)
+        cache_f[:rows_of, :] = cache[t * rows_of : (t + 1) * rows_of, :].astype(F32)
         for kind in range(2):
             for h in range(kv_heads):
                 split[t, kind, h // 2, :, h % 2 * head_dim : (h % 2 + 1) * head_dim] = cache_f[
@@ -451,7 +451,9 @@
             MIXED, mixed_out, mixed_in.at[et_peer(i)], et_peer(i)
         ).wait_recv(),
     )
-    mixed_f[...] = mixed_in[...].reshape(tokens * n_heads, head_dim).astype(F32)
+    mixed_f[: tokens * n_heads, :] = (
+        mixed_in[...].reshape(tokens * n_heads, head_dim).astype(F32)
+    )
     attended = jnp.concatenate(
         [mixed_f[pl.ds(h, tokens, stride=n_heads), :] for h in range(n_heads)], axis=1
     ).astype(BF16)
@@ -688,19 +690,19 @@
     chunk = 2 * n_local * CAP
     vmem = pltpu.VMEM
     row_blocks = (n_stream, chunk, LANES)
-    flat_rows = (n_stream * chunk, LANES)
+    flat_rows = ((n_stream + 1) * chunk, LANES)
     parts = parts_of(n_stream)
     n_waves = parts // 2
     share, small = n_stream // n_waves, n_stream // parts
     scratch = [vmem(a.shape, a.dtype) for a in args[1:]] + [
-        vmem((span * kv_heads * 2, head_dim), F32),
+        vmem(((span + 1) * kv_heads * 2, head_dim), F32),
         vmem((local, 2, kv_heads // 2, span, 2 * head_dim), BF16),
         vmem((n_et, tokens, features), BF16),
         vmem((n_et, 16, head_dim), BF16),
         vmem((n_et, 16, head_dim), BF16),
         vmem((local * n_heads, head_dim), BF16),
         vmem((n_et, local * n_heads, head_dim), BF16),
-        vmem((tokens * n_heads, head_dim), F32),
+        vmem(((tokens + 1) * n_heads, head_dim), F32),
         vmem(row_blocks, BF16),
         vmem(row_blocks, BF16),
         vmem(flat_rows, F32),

time: 53.1 us -> 53.1 us (level)
  no operation moved by 1% of the time
where the time goes in v10:
time: 53.1 us; the launch traced here: 53 us
  Pallas kernels  52.4 us (99%)
  local copies, waits for them, and re-layouts  0.6 us (1%)
    pallas_call x1, Pallas kernels, on_device(): pl.pallas_call(functools.partial(kernel, n_stream, n_et), out_shape=pltpu...  52.4 us

profile of v10, /device:TPU:1, one launch (start us, length us, event | category | flops | bytes accessed | tf_op | source)
XLA Modules:
  0.0 53.0 jit_solution(15608217977336638841)
XLA Ops:
  0.0 52.4 %shard_map.136 = bf16[16,256]{1,0:T(8,128)(2,1)S(1)} custom-call(bf16[16,256]{1,0:T(8,128)(2,1)} %res_hbm.1, bf16[16,128]{1,0:T(8,128)(2,1)} %bitcast.13, bf16[1,128]{1,0:T(2,128)(2,1)} %bitcast.16, bf16[1,128]{1,0:T(2,128)(2,1)} %bitcast.17, bf16[2048,512]{1,0:T(8,128)(2,1)} %w_q_hbm.1, bf16[2048,128]{1,0:T(8,128)(2,1)} %w_kv_hbm.1, ...), custom_call_target="tpu_custom_call" | custom-call | tf_op jit(solution)/shard_map/pallas_call | solution.py:728
  52.4 0.6 %copy.17 = bf16[16,256]{1,0:T(8,128)(2,1)} copy(bf16[16,256]{1,0:T(8,128)(2,1)S(1)} %shard_map.136) | data formatting | bytes 16384

commit v11 on v10

--- a/solution.py
+++ b/solution.py
@@ -582,7 +582,8 @@
             .astype(BF16)
             .reshape(share, chunk, LANES)
         )
-        for part in (2 * w, 2 * w + 1):
+        ahead = lax.rem(own_part + jnp.where(lax.div(own_part, 2) == w, 1, 0), 2)
+        for part in (2 * w + ahead, 2 * w + 1 - ahead):
             *rest, (last, place) = members(part)
             for number, (peer, slot) in enumerate(rest):
                 stream_copy(

time: 53.1 us -> 53.1 us (level)
  no operation moved by 1% of the time
where the time goes in v11:
time: 53.1 us; the launch traced here: 53 us
  Pallas kernels  52.4 us (99%)
  local copies, waits for them, and re-layouts  0.6 us (1%)
    pallas_call x1, Pallas kernels, on_device(): pl.pallas_call(functools.partial(kernel, n_stream, n_et), out_shape=pltpu...  52.4 us

profile of v11, /device:TPU:1, one launch (start us, length us, event | category | flops | bytes accessed | tf_op | source)
XLA Modules:
  0.0 53.0 jit_solution(1264745140713279074)
XLA Ops:
  0.0 52.4 %shard_map.136 = bf16[16,256]{1,0:T(8,128)(2,1)S(1)} custom-call(bf16[16,256]{1,0:T(8,128)(2,1)} %res_hbm.1, bf16[16,128]{1,0:T(8,128)(2,1)} %bitcast.13, bf16[1,128]{1,0:T(2,128)(2,1)} %bitcast.16, bf16[1,128]{1,0:T(2,128)(2,1)} %bitcast.17, bf16[2048,512]{1,0:T(8,128)(2,1)} %w_q_hbm.1, bf16[2048,128]{1,0:T(8,128)(2,1)} %w_kv_hbm.1, ...), custom_call_target="tpu_custom_call" | custom-call | tf_op jit(solution)/shard_map/pallas_call | solution.py:729
  52.4 0.6 %copy.17 = bf16[16,256]{1,0:T(8,128)(2,1)} copy(bf16[16,256]{1,0:T(8,128)(2,1)S(1)} %shard_map.136) | data formatting | bytes 16384
